TPU v7x, 128 devices: a whole 4x4x4 slice. The times are simulated.
128 devices in a mesh: member: 16 (over z, x_lo, core), fsdp: 8 (over x_hi, y).
Axes of the slice: x: 4 (x_hi: 2, x_lo: 2; x = x_hi * 2 + x_lo), y: 4, z: 4, core: 2. Of those that a mesh axis runs over, the one named last changes fastest.
Arguments:
- hidden: bfloat16 [16, 3072, 3584], P('member', 'fsdp'), may hold values from -6 to 6
- value_grad: bfloat16 [16, 3072, 2048], P('member', 'fsdp'), may hold values from -1.796875 to 1.796875
- weight: bfloat16 [16, 3584, 2048], P('member', 'fsdp'), may hold values from -0.09375 to 0.09375
- moment_one: bfloat16 [16, 3584, 2048], P('member', 'fsdp'), may hold values from -6 to 6
- moment_two: bfloat16 [16, 3584, 2048], P('member', 'fsdp'), may hold values from 0.5 to 8
- norm_gain: float32 [16, 3584], P('member'), may hold values from -0.5 to 0.5
- gain_first: float32 [16, 3584], P('member'), may hold values from -6 to 6
- gain_second: float32 [16, 3584], P('member'), may hold values from 0.3 to 10
- donors: int32 [16], replicated, may hold values from 0 to 15
- recipient: int32 [16], replicated, may hold values 0 or 1
Outputs:
- values: bfloat16 [16, 3072, 2048], P('member', 'fsdp')
- hidden_grad: bfloat16 [16, 3072, 3584], P('member', 'fsdp')
- weight_out: bfloat16 [16, 3584, 2048], P('member', 'fsdp')
- first_out: bfloat16 [16, 3584, 2048], P('member', 'fsdp')
- second_out: bfloat16 [16, 3584, 2048], P('member', 'fsdp')
- gain_out: float32 [16, 3584], P('member')
- gain_first_out: float32 [16, 3584], P('member')
- gain_second_out: float32 [16, 3584], P('member')
All inputs are finite; a program needn't handle non-finite values.
Results may differ from a plain program's by a relative error of at most 0.015.
Values may be sent and summed in bfloat16 or wider, within the bound.
No kernel may reach another device: no remote copies, remote signals or barrier semaphores. Data moves between devices by JAX's collectives and lax.ppermute only.
A program may use at most 192 MiB of HBM per device.

v0:
```python
import jax
import jax.numpy as jnp
from jax import lax
from jax.sharding import PartitionSpec as P

STEP = 100


beta_one = 0.9
beta_two = 0.999
adam_eps = 1e-08
learn_rate = 0.001
decay_rate = 0.1
norm_eps = 1e-06


def adam_update(param, grad, first, second, decay):
    first_new = beta_one * first + (1.0 - beta_one) * grad
    second_new = beta_two * second + (1.0 - beta_two) * grad * grad
    corr_one = 1.0 - beta_one**STEP
    corr_two = 1.0 - beta_two**STEP
    step_dir = first_new / corr_one / (jnp.sqrt(second_new / corr_two) + adam_eps) + decay * param
    return (param - learn_rate * step_dir, first_new, second_new)


def shards(
    hidden,
    value_grad,
    weight,
    moment_one,
    moment_two,
    norm_gain,
    gain_first,
    gain_second,
    donors,
    recipient,
):
    tokens_in = hidden[0]
    cotangent = value_grad[0]
    wide = tokens_in.astype(jnp.float32)
    scale = lax.rsqrt(jnp.mean(wide * wide, axis=-1, keepdims=True) + norm_eps)
    normed = wide * scale
    factor = 1.0 + norm_gain[0]
    inputs = (normed * factor).astype(jnp.bfloat16)
    full_weight = lax.all_gather(weight, "fsdp", axis=1, tiled=True)[0]
    values = jnp.dot(inputs, full_weight, preferred_element_type=jnp.float32).astype(jnp.bfloat16)
    input_grad = lax.dot_general(
        cotangent, full_weight, (((1,), (1,)), ((), ())), preferred_element_type=jnp.float32
    )
    gain_grad = lax.psum(jnp.sum(input_grad * normed, axis=0), "fsdp")
    scaled = input_grad * factor
    hidden_grad = (
        scale * (scaled - normed * jnp.mean(scaled * normed, axis=-1, keepdims=True))
    ).astype(jnp.bfloat16)
    weight_grad = lax.psum_scatter(
        lax.dot_general(
            inputs, cotangent, (((0,), (0,)), ((), ())), preferred_element_type=jnp.float32
        ).astype(jnp.bfloat16),
        "fsdp",
        scatter_dimension=0,
        tiled=True,
    ).astype(jnp.float32)
    updated, first, second = adam_update(
        weight[0].astype(jnp.float32),
        weight_grad,
        moment_one[0].astype(jnp.float32),
        moment_two[0].astype(jnp.float32),
        decay_rate,
    )
    new_gain, new_first, new_second = adam_update(
        norm_gain[0], gain_grad, gain_first[0], gain_second[0], 0.0
    )
    members = lax.axis_size("member")
    own_index = jnp.arange(members, dtype=jnp.int32)
    source = jnp.where(recipient == 1, donors, own_index)
    selector = (source[:, None] == own_index[None, :]).astype(jnp.bfloat16)
    state_w = updated.astype(jnp.bfloat16)[None]
    state_m = first.astype(jnp.bfloat16)[None]
    state_v = second.astype(jnp.bfloat16)[None]
    states = (
        lax.all_to_all(state_w, "member", split_axis=2, concat_axis=0, tiled=True),
        lax.all_to_all(state_m, "member", split_axis=2, concat_axis=0, tiled=True),
        lax.all_to_all(state_v, "member", split_axis=2, concat_axis=0, tiled=True),
    )
    picked = tuple(
        (
            jnp.einsum("rs,sxc->rxc", selector, item, preferred_element_type=jnp.float32).astype(
                jnp.bfloat16
            )
            for item in states
        )
    )
    weight_out = lax.all_to_all(picked[0], "member", split_axis=0, concat_axis=2, tiled=True)
    first_out = lax.all_to_all(picked[1], "member", split_axis=0, concat_axis=2, tiled=True)
    second_out = lax.all_to_all(picked[2], "member", split_axis=0, concat_axis=2, tiled=True)
    all_gain, all_first, all_second = (
        lax.all_gather(new_gain[None], "member", axis=0, tiled=True),
        lax.all_gather(new_first[None], "member", axis=0, tiled=True),
        lax.all_gather(new_second[None], "member", axis=0, tiled=True),
    )
    my_source = source[lax.axis_index("member")]
    pick = (own_index == my_source).astype(jnp.float32)[:, None]
    gain_out = jnp.sum(pick * all_gain, axis=0)[None]
    gain_first_out = jnp.sum(pick * all_first, axis=0)[None]
    gain_second_out = jnp.sum(pick * all_second, axis=0)[None]
    return (
        values[None],
        hidden_grad[None],
        weight_out,
        first_out,
        second_out,
        gain_out,
        gain_first_out,
        gain_second_out,
    )


def solution(mesh):
    in_specs = (
        P("member", "fsdp", None),
        P("member", "fsdp", None),
        P("member", "fsdp", None),
        P("member", "fsdp", None),
        P("member", "fsdp", None),
        P("member", None),
        P("member", None),
        P("member", None),
        P(),
        P(),
    )
    out_specs = (
        P("member", "fsdp", None),
        P("member", "fsdp", None),
        P("member", "fsdp", None),
        P("member", "fsdp", None),
        P("member", "fsdp", None),
        P("member", None),
        P("member", None),
        P("member", None),
    )
    return jax.shard_map(shards, mesh=mesh, in_specs=in_specs, out_specs=out_specs, check_vma=False)
```

profile of v0, /device:TPU:1, one launch (start us, length us, event | category | flops | bytes accessed | tf_op | source)
XLA Modules:
  0.0 617.8 jit_solution(6287503893611956473)
XLA Ops:
  10.9 11.3 %convolution_convert_fusion = bf16[3584,2048]{1,0:T(8,128)(2,1)} fusion(bf16[1,384,2048]{2,1,0:T(8,128)(2,1)S(1)} %copy-done, bf16[1,384,3584]{2,1,0:T(8,128)(2,1)S(1)} %copy-done.2, f32[3584]{0:T(1024)S(1)} %get-tuple-element.11, f32[384]{0:T(512)S(1)} %add_rsqrt_fusion), kind=kOutput, calls=%fused_computation | convolution fusion | flops 5649989632 | bytes 19021312 | tf_op jit(solution)/shard_map/dot_general | solution.py:56
  23.0 171.5 %reduce-scatter.2.cloned.1.call-done = bf16[448,2048]{1,0:T(8,128)(2,1)} async-done(((bf16[3584,2048]{1,0:T(8,128)(2,1)}), bf16[448,2048]{1,0:T(8,128)(2,1)}) %reduce-scatter.2.cloned.1.call-update) | async-done | bytes 1835024 | tf_op jit(solution)/shard_map/reduce_scatter | solution.py:55
  194.4 7.6 %fusion.32 = (bf16[1,448,2048]{2,1,0:T(8,128)(2,1)}, bf16[1,448,2048]{2,1,0:T(8,128)(2,1)}, bf16[1,448,2048]{2,1,0:T(8,128)(2,1)}) fusion(bf16[448,2048]{1,0:T(8,128)(2,1)} %reduce-scatter.2.cloned.1.call-done, bf16[1,448,2048]{2,1,0:T(8,128)(2,1)} %param.14, bf16[1,448,2048]{2,1,0:T(8,128)(2,1)} %param.13, bf16[1,448,2048]{2,1,0:T(8,128)(2,1)S(1)} %copy-done.3), kind=kLoop, calls=%fused_computation.35 | loop fusion | flops 20185088 | bytes 12845056 | tf_op jit(solution)/shard_map/broadcast_in_dim | solution.py:79
  202.1 10.9 %copy.27 = bf16[1,448,2048]{1,0,2:T(2,128)(2,1)} copy(bf16[1,448,2048]{2,1,0:T(8,128)(2,1)} %get-tuple-element.19) | data formatting | bytes 3670016 | tf_op jit(solution)/shard_map/broadcast_in_dim | solution.py:77
  213.5 15.4 %reduce.8 = bf16[2048,448]{1,0:T(8,128)(2,1)} reduce(bf16[2048,1,448]{2,1,0:T(2,128)(2,1)} %bitcast.155, bf16[]{:T(256)} %broadcast.87), dimensions={1}, to_apply=%bitcast.139.reduce_sub_computation | reduce | bytes 3670018
  228.9 5.8 reshape.98
  234.7 6.1 all-to-all-start
  240.9 7.5 %copy.31 = bf16[1,448,2048]{1,0,2:T(2,128)(2,1)} copy(bf16[1,448,2048]{2,1,0:T(8,128)(2,1)S(1)} %copy-done.5) | data formatting | bytes 3670016 | tf_op jit(solution)/shard_map/broadcast_in_dim | solution.py:78
  248.4 15.4 %reduce.9 = bf16[2048,448]{1,0:T(8,128)(2,1)} reduce(bf16[2048,1,448]{2,1,0:T(2,128)(2,1)} %bitcast.157, bf16[]{:T(256)} %broadcast.87), dimensions={1}, to_apply=%bitcast.141.reduce_sub_computation | reduce | bytes 3670018
  263.8 5.8 reshape.100
  272.5 6.0 all-to-all-start.2
  278.5 7.5 %copy.35 = bf16[1,448,2048]{1,0,2:T(2,128)(2,1)} copy(bf16[1,448,2048]{2,1,0:T(8,128)(2,1)S(1)} %copy-done.4) | data formatting | bytes 3670016 | tf_op jit(solution)/shard_map/broadcast_in_dim | solution.py:79
  286.0 15.4 %reduce.10 = bf16[2048,448]{1,0:T(8,128)(2,1)} reduce(bf16[2048,1,448]{2,1,0:T(2,128)(2,1)} %bitcast.156, bf16[]{:T(256)} %broadcast.87), dimensions={1}, to_apply=%bitcast.143.reduce_sub_computation | reduce | bytes 3670018
  301.5 5.8 reshape.102
  307.3 15.5 %all-to-all-done.2 = bf16[16,2,28672]{2,1,0:T(2,128)(2,1)} async-done(((bf16[16,2,28672]{2,1,0:T(2,128)(2,1)}), bf16[16,2,28672]{2,1,0:T(2,128)(2,1)}, u32[]{:S(2)}, u32[]{:S(2)}) %all-to-all-start.2) | async-done | bytes 1835040 | tf_op jit(solution)/shard_map/all_to_all | solution.py:82
  322.8 4.4 all-to-all-start.4
  328.6 10.8 %reshape.99 = bf16[2048,1,448]{2,1,0:T(2,128)(2,1)} reshape(bf16[16,2,28672]{2,1,0:T(2,128)(2,1)} %all-to-all-done) | data formatting | bytes 3670016
  343.4 4.4 copy.39
  351.7 19.7 %all-to-all-done.4 = bf16[16,2,28672]{2,1,0:T(2,128)(2,1)S(1)} async-done(((bf16[16,2,28672]{2,1,0:T(2,128)(2,1)}), bf16[16,2,28672]{2,1,0:T(2,128)(2,1)S(1)}, u32[]{:S(2)}, u32[]{:S(2)}) %all-to-all-start.4) | async-done | bytes 1835040 | tf_op jit(solution)/shard_map/all_to_all | solution.py:83
  372.7 4.6 all-to-all-start.1
  377.3 32.4 %all-gather.8.cloned.1.call-done = bf16[1,3584,2048]{2,1,0:T(8,128)(2,1)} async-done(((bf16[1,448,2048]{2,1,0:T(8,128)(2,1)}), bf16[1,3584,2048]{2,1,0:T(8,128)(2,1)}) %all-gather.8.cloned.1.call-update) | async-done | bytes 14680080 | tf_op jit(solution)/shard_map/all_gather | solution.py:45
  409.7 11.6 %fusion.13 = (f32[3584]{0:T(1024)S(1)}, f32[384]{0:T(512)S(1)}, f32[384,3584]{1,0:T(8,128)}) fusion(bf16[1,384,3584]{2,1,0:T(8,128)(2,1)} %param.10, f32[384]{0:T(512)S(1)} %add_rsqrt_fusion, f32[3584]{0:T(1024)S(1)} %get-tuple-element.11, bf16[1,3584,2048]{2,1,0:T(8,128)(2,1)} %all-gather.8.cloned.1.call-done, bf16[1,384,2048]{2,1,0:T(8,128)(2,1)S(1)} %copy-done), kind=kOutput, calls=%fused_computation.16 | convolution fusion | flops 5646774272 | bytes 24542208 | tf_op jit(solution)/shard_map/dot_general | solution.py:47
  421.3 30.4 %psum.7 = f32[3584]{0:T(1024)S(1)} all-reduce(f32[3584]{0:T(1024)S(1)} %get-tuple-element.8), channel_id=1, replica_groups=mesh['member'=16,'fsdp'=8] {'fsdp'}, use_global_device_ids=true, to_apply=%region_4.0 | all-reduce | flops 3584 | bytes 28672 | tf_op jit(solution)/shard_map/psum | solution.py:50
  451.8 26.1 %all-gather.5 = f32[16,1,3584]{2,1,0:T(1,128)S(1)} all-gather(f32[1,1,3584]{2,1,0:T(1,128)S(1)} %reshape.85), channel_id=4, replica_groups=mesh['member'=16,'fsdp'=8] {'member'}, dimensions={0}, use_global_device_ids=true | all-gather | bytes 243712 | tf_op jit(solution)/shard_map/all_gather | solution.py:99
  477.9 17.5 %all-gather.4 = f32[16,1,3584]{2,1,0:T(1,128)S(1)} all-gather(f32[1,1,3584]{2,1,0:T(1,128)S(1)} %reshape.83), channel_id=3, replica_groups=mesh['member'=16,'fsdp'=8] {'member'}, dimensions={0}, use_global_device_ids=true | all-gather | bytes 243712 | tf_op jit(solution)/shard_map/all_gather | solution.py:98
  495.4 18.2 %all-gather.3 = f32[16,1,3584]{2,1,0:T(1,128)S(1)} all-gather(f32[1,1,3584]{2,1,0:T(1,128)S(1)} %reshape.81), channel_id=2, replica_groups=mesh['member'=16,'fsdp'=8] {'member'}, dimensions={0}, use_global_device_ids=true | all-gather | bytes 243712 | tf_op jit(solution)/shard_map/all_gather | solution.py:97
  515.6 10.7 %reshape.101 = bf16[2048,1,448]{2,1,0:T(2,128)(2,1)} reshape(bf16[16,2,28672]{2,1,0:T(2,128)(2,1)} %all-to-all-done.2) | data formatting | bytes 3670016
  543.0 10.9 %fusion.29 = bf16[1,384,2048]{2,1,0:T(8,128)(2,1)} fusion(bf16[1,3584,2048]{2,1,0:T(8,128)(2,1)} %all-gather.8.cloned.1.call-done, bf16[1,384,3584]{2,1,0:T(8,128)(2,1)} %param.10, f32[3584]{0:T(1024)S(1)} %get-tuple-element.11, f32[384]{0:T(512)S(1)} %add_rsqrt_fusion), kind=kOutput, calls=%fused_computation.34 | convolution fusion | flops 5643436032 | bytes 19021312 | tf_op jit(solution)/shard_map/dot_general | solution.py:46
  553.9 10.7 %reshape.103 = bf16[2048,1,448]{2,1,0:T(2,128)(2,1)} reshape(bf16[16,2,28672]{2,1,0:T(2,128)(2,1)} %copy-done.6) | data formatting | bytes 3670016
  577.1 6.2 all-to-all-start.5
  583.3 6.6 %fusion.28 = bf16[1,384,3584]{2,1,0:T(8,128)(2,1)} fusion(bf16[1,384,3584]{2,1,0:T(8,128)(2,1)} %param.10, f32[384,3584]{1,0:T(8,128)} %get-tuple-element.21, f32[384]{0:T(512)S(1)} %broadcast_multiply_fusion, f32[3584]{0:T(1024)S(1)} %get-tuple-element.11, f32[384]{0:T(512)S(1)} %add_rsqrt_fusion), kind=kLoop, calls=%fused_computation.33 | loop fusion | flops 9633792 | bytes 11027456 | tf_op jit(solution)/shard_map/broadcast_in_dim | solution.py:108
  594.5 13.0 %all-to-all-done.5 = bf16[16,448,128]{2,1,0:T(8,128)(2,1)} async-done(((bf16[16,448,128]{2,1,0:T(8,128)(2,1)}), bf16[16,448,128]{2,1,0:T(8,128)(2,1)}, u32[]{:S(2)}, u32[]{:S(2)}) %all-to-all-start.5) | async-done | bytes 1835040 | tf_op jit(solution)/shard_map/all_to_all | solution.py:95
  (61 shorter events, 57.3 us)
Async XLA Ops:
  7.2 3.7 copy-start
  7.2 187.2 %reduce-scatter.2.cloned.1.call-start = ((), (), s32[]{:S(2)}) async-start(), calls=%async_computation.8 | async-start | bytes 16515072 | tf_op jit(solution)/shard_map/reduce_scatter | solution.py:55
  7.2 3.7 copy-start.2
  22.2 172.2 %copy-start.3 = (bf16[1,448,2048]{2,1,0:T(8,128)(2,1)S(1)}, bf16[1,448,2048]{2,1,0:T(8,128)(2,1)}, u32[]{:S(2)}) copy-start(bf16[1,448,2048]{2,1,0:T(8,128)(2,1)} %param.12) | copy-start | bytes 5505028
  22.2 387.5 %all-gather.8.cloned.1.call-start = ((), (), s32[]{:S(2)}) async-start(), calls=%async_computation.7 | async-start | bytes 16515072 | tf_op jit(solution)/shard_map/all_gather | solution.py:45
  234.7 6.1 copy-start.5
  234.7 37.8 %all-to-all-start = ((bf16[16,2,28672]{2,1,0:T(2,128)(2,1)}), bf16[16,2,28672]{2,1,0:T(2,128)(2,1)}, u32[]{:S(2)}, u32[]{:S(2)}) async-start(bf16[16,2,28672]{2,1,0:T(2,128)(2,1)} %reshape.98), calls=%async_computation.1 | async-start | bytes 3670016 | tf_op jit(solution)/shard_map/all_to_all | solution.py:81
  269.6 8.9 %copy-start.4 = (bf16[1,448,2048]{2,1,0:T(8,128)(2,1)S(1)}, bf16[1,448,2048]{2,1,0:T(8,128)(2,1)}, u32[]{:S(2)}) copy-start(bf16[1,448,2048]{2,1,0:T(8,128)(2,1)} %get-tuple-element.18) | copy-start | bytes 5505028
  272.5 50.2 %all-to-all-start.2 = ((bf16[16,2,28672]{2,1,0:T(2,128)(2,1)}), bf16[16,2,28672]{2,1,0:T(2,128)(2,1)}, u32[]{:S(2)}, u32[]{:S(2)}) async-start(bf16[16,2,28672]{2,1,0:T(2,128)(2,1)} %reshape.100), calls=%async_computation.3 | async-start | bytes 3670016 | tf_op jit(solution)/shard_map/all_to_all | solution.py:82
  307.2 19.9 %copy-start.9 = (s32[16]{0:T(128)S(1)}, s32[16]{0:T(128)}, u32[]{:S(2)}) copy-start(s32[16]{0:T(128)} %param.18) | copy-start | bytes 196
  307.2 19.9 %copy-start.10 = (s32[16]{0:T(128)S(1)}, s32[16]{0:T(128)}, u32[]{:S(2)}) copy-start(s32[16]{0:T(128)} %param.19) | copy-start | bytes 196
  307.2 21.2 %copy-start.7 = (f32[1,3584]{1,0:T(1,128)S(1)}, f32[1,3584]{1,0:T(1,128)}, u32[]{:S(2)}) copy-start(f32[1,3584]{1,0:T(1,128)} %param.17) | copy-start | bytes 43012
  307.2 21.2 %copy-start.8 = (f32[1,3584]{1,0:T(1,128)S(1)}, f32[1,3584]{1,0:T(1,128)}, u32[]{:S(2)}) copy-start(f32[1,3584]{1,0:T(1,128)} %param.16) | copy-start | bytes 43012
  322.8 48.7 %all-to-all-start.4 = ((bf16[16,2,28672]{2,1,0:T(2,128)(2,1)}), bf16[16,2,28672]{2,1,0:T(2,128)(2,1)S(1)}, u32[]{:S(2)}, u32[]{:S(2)}) async-start(bf16[16,2,28672]{2,1,0:T(2,128)(2,1)} %reshape.102), calls=%async_computation.5 | async-start | bytes 3670016 | tf_op jit(solution)/shard_map/all_to_all | solution.py:83
  371.4 1.2 copy-start.6
  372.7 166.1 %all-to-all-start.1 = ((bf16[16,448,128]{2,1,0:T(8,128)(2,1)}), bf16[16,448,128]{2,1,0:T(8,128)(2,1)S(1)}, u32[]{:S(2)}, u32[]{:S(2)}) async-start(bf16[16,448,128]{2,1,0:T(8,128)(2,1)} %copy.29), calls=%async_computation.2 | async-start | bytes 3670016 | tf_op jit(solution)/shard_map/all_to_all | solution.py:93
  538.7 38.4 %all-to-all-start.3 = ((bf16[16,448,128]{2,1,0:T(8,128)(2,1)}), bf16[16,448,128]{2,1,0:T(8,128)(2,1)}, u32[]{:S(2)}, u32[]{:S(2)}) async-start(bf16[16,448,128]{2,1,0:T(8,128)(2,1)} %copy.33), calls=%async_computation.4 | async-start | bytes 3670016 | tf_op jit(solution)/shard_map/all_to_all | solution.py:94
  577.1 30.4 %all-to-all-start.5 = ((bf16[16,448,128]{2,1,0:T(8,128)(2,1)}), bf16[16,448,128]{2,1,0:T(8,128)(2,1)}, u32[]{:S(2)}, u32[]{:S(2)}) async-start(bf16[16,448,128]{2,1,0:T(8,128)(2,1)} %copy.37), calls=%async_computation.6 | async-start | bytes 3670016 | tf_op jit(solution)/shard_map/all_to_all | solution.py:95
  591.3 19.2 %copy-start.1 = (bf16[1,384,2048]{2,1,0:T(8,128)(2,1)S(1)}, bf16[1,384,2048]{2,1,0:T(8,128)(2,1)}, u32[]{:S(2)}) copy-start(bf16[1,384,2048]{2,1,0:T(8,128)(2,1)} %param.11) | copy-start | bytes 4718596
Sparse Core Ops, SparseCore 0:
  22.3 172.0 reduce-scatter.1
  196.7 212.8 all-gather.7
where the time goes:
time: 628 us; the launch traced here: 618 us
  waiting for transfers between devices  256 us (41%)
  local copies, waits for them, and re-layouts  118 us (19%)
  blocking collectives  92.2 us (15%)
  other arithmetic  65.1 us (10%)
  matrix products  40.3 us (6%)
  starting transfers between devices  31.7 us (5%)
  between operations  14.7 us (2%)
    reduce_scatter x1, waiting for transfers between devices, shards(): lax.psum_scatter(lax.dot_general(inputs, cotangent, (((0,), (0,)), ((), (...  171 us
    unnamed x35, local copies, waits for them, and re-layouts  63.7 us
    unnamed x4, other arithmetic  47.2 us
    all_gather x1, waiting for transfers between devices, shards(): full_weight = lax.all_gather(weight, 'fsdp', axis=1, tiled=True)[0]  32.4 us
    psum x1, blocking collectives, shards(): gain_grad = lax.psum(jnp.sum(input_grad * normed, axis=0), 'fsdp')  30.4 us
    all_gather x1, blocking collectives, shards(): lax.all_gather(new_second[None], 'member', axis=0, tiled=True)  26.1 us
    all_to_all x1, waiting for transfers between devices, shards(): lax.all_to_all(state_v, 'member', split_axis=2, concat_axis=0, tiled=True)  19.7 us
    all_gather x1, blocking collectives, shards(): lax.all_gather(new_gain[None], 'member', axis=0, tiled=True)  18.2 us
  transfers between devices with their start and end apart: 8, of which 6 were waited for; matrix products, arithmetic and copies ran while one was open for 33% of the time, Pallas kernels for 0%

commit v1 on v0

v1 whole, which is shorter than its diff:
```python
import functools

import jax
import jax.numpy as jnp
from jax import lax
from jax.experimental import pallas as pl
from jax.experimental.pallas import tpu as pltpu
from jax.sharding import PartitionSpec as P

STEP = 100
beta_one = 0.9
beta_two = 0.999
adam_eps = 1e-08
learn_rate = 0.001
decay_rate = 0.1
norm_eps = 1e-06

BF16 = jnp.bfloat16
F32 = jnp.float32
CHUNKS = 2
SLOTS = 3

Y_GROUPS = [[0, 1, 2, 3], [4, 5, 6, 7]]
X_GROUPS = [[p // 2 * 4 + x * 2 + p % 2 for p in range(8)] for x in range(2)]
PARAMS = pltpu.CompilerParams(vmem_limit_bytes=56 * 1024 * 1024)
STORE_PARAMS = pltpu.CompilerParams(vmem_limit_bytes=16 * 1024 * 1024)


def adam_update(param, grad, first, second, decay):
    first_new = beta_one * first + (1.0 - beta_one) * grad
    second_new = beta_two * second + (1.0 - beta_two) * grad * grad
    corr_one = 1.0 - beta_one**STEP
    corr_two = 1.0 - beta_two**STEP
    step_dir = first_new / corr_one / (jnp.sqrt(second_new / corr_two) + adam_eps) + decay * param
    return (param - learn_rate * step_dir, first_new, second_new)


def to_fsdp(x, dx=0, dy=0):
    pairs = [(f, ((f // 4) ^ dx) * 4 + (f % 4 + dy) % 4) for f in range(8)]
    return lax.ppermute(x, "fsdp", pairs)


def to_member(x, dz=0, dx=0, dc=0):
    pairs = [
        (m, ((m // 4 + dz) % 4) * 4 + ((m // 2 % 2) ^ dx) * 2 + ((m % 2) ^ dc)) for m in range(16)
    ]
    return lax.ppermute(x, "member", pairs)


def swap_members(x):
    return lax.all_to_all(x, "member", 0, 0, axis_index_groups=X_GROUPS)


def pick(x, index, axis=0):
    return lax.dynamic_index_in_dim(x, index, axis, keepdims=False)


def tie(x, *others):
    return lax.optimization_barrier((x, others))[0]


def put(x, part, index, axis=0):
    return lax.dynamic_update_index_in_dim(x, part, index, axis)


def matmul(a, b, contract):
    return lax.dot_general(a, b, ((contract[:1], contract[1:]), ((), ())), preferred_element_type=F32)


SMALL = pl.CostEstimate(flops=0, bytes_accessed=65536, transcendentals=0)
LARGE = pl.CostEstimate(flops=20_000_000_000, bytes_accessed=10_000_000, transcendentals=0)
ANYWHERE = pl.BlockSpec(memory_space=pl.ANY)


def split_kernel(xh_ref, hidden_ref, gain_ref, out_ref):
    wide = hidden_ref[...].astype(F32)
    scale = lax.rsqrt(jnp.mean(wide * wide, axis=-1, keepdims=True) + norm_eps)
    full = wide * scale * (1.0 + gain_ref[...])
    half = full.shape[1] // 2
    rows = half // 4
    low, high = full[:, :half], full[:, half:]
    swap = xh_ref[0] == 1
    first, second = jnp.where(swap, high, low), jnp.where(swap, low, high)
    for q in range(4):
        part = slice(q * rows, (q + 1) * rows)
        out_ref[q] = jnp.concatenate([first[:, part], second[:, part]], axis=1).astype(BF16)


def split_inputs(hidden, gain, xh):
    tokens, features = hidden.shape
    step = 96
    return pl.pallas_call(
        split_kernel,
        grid_spec=pltpu.PrefetchScalarGridSpec(
            num_scalar_prefetch=1,
            grid=(tokens // step,),
            in_specs=[
                pl.BlockSpec((step, features), lambda i, s: (i, 0)),
                pl.BlockSpec((1, features), lambda i, s: (0, 0)),
            ],
            out_specs=pl.BlockSpec((4, step, features // 4), lambda i, s: (0, i, 0)),
        ),
        out_shape=jax.ShapeDtypeStruct((4, tokens, features // 4), BF16),
        compiler_params=PARAMS,
        cost_estimate=SMALL,
        name="split_inputs",
    )(xh[None], hidden, gain)


def join_kernel(place_ref, hidden_ref, gain_ref, *refs):
    ins, value_refs, (out_ref, values_ref) = refs[:4], refs[4:9], refs[9:]
    xh, y = place_ref[0], place_ref[1]
    total = value_refs[0][...].astype(F32)
    for ref in value_refs[1:3]:
        total = total + ref[...].astype(F32)
    half = total.shape[1] // 2
    for k, ref in enumerate(value_refs[3:]):
        at = slice(k * half, (k + 1) * half)
        values_ref[:, at] = (total[:, at] + ref[...].astype(F32)).astype(BF16)
    wide = hidden_ref[...].astype(F32)
    scale = lax.rsqrt(jnp.mean(wide * wide, axis=-1, keepdims=True) + norm_eps)
    normed = wide * scale
    rows = ins[0].shape[1] // 2
    came = [ref[...].astype(F32) for ref in ins]
    parts = []
    for q in range(4):
        d = lax.rem(y + (4 - q), 4)
        part = came[0]
        for k in (1, 2, 3):
            part = jnp.where(d == k, came[k], part)
        parts.append(part)
    first = jnp.concatenate([p[:, :rows] for p in parts], axis=1)
    second = jnp.concatenate([p[:, rows:] for p in parts], axis=1)
    swap = xh == 1
    grad = jnp.concatenate([jnp.where(swap, second, first), jnp.where(swap, first, second)], axis=1)
    scaled = grad * (1.0 + gain_ref[...])
    mean = jnp.mean(scaled * normed, axis=-1, keepdims=True)
    out_ref[...] = (scale * (scaled - normed * mean)).astype(BF16)


def join_parts(hidden, gain, parts, values, xh, y):
    tokens, features = hidden.shape
    step = 96
    row = lambda i, s: (i, 0)
    return pl.pallas_call(
        join_kernel,
        grid_spec=pltpu.PrefetchScalarGridSpec(
            num_scalar_prefetch=1,
            grid=(tokens // step,),
            in_specs=[
                pl.BlockSpec((step, features), row),
                pl.BlockSpec((1, features), lambda i, s: (0, 0)),
            ]
            + [pl.BlockSpec((step, features // 4), row)] * 4
            + [pl.BlockSpec((step, value.shape[1]), row) for value in values],
            out_specs=[
                pl.BlockSpec((step, features), row),
                pl.BlockSpec((step, values[0].shape[1]), row),
            ],
        ),
        out_shape=[
            jax.ShapeDtypeStruct((tokens, features), BF16),
            jax.ShapeDtypeStruct(values[0].shape, BF16),
        ],
        compiler_params=PARAMS,
        cost_estimate=LARGE,
        name="join_parts",
    )(jnp.stack([xh, y]), hidden, gain, *parts, *values)


def spread_kernel(*refs):
    ins, outs = refs[:3], refs[3:]
    cc = outs[0].shape[3]
    for i, out_ref in enumerate(outs):
        for g in range(2):
            at = (2 * i + g) * cc
            for k in range(3):
                out_ref[g, k] = ins[k][:, at : at + cc]


def spread_states(arrays):
    rows, width = arrays[0].shape
    part, cc = rows // 4, width // CHUNKS // 2
    return pl.pallas_call(
        spread_kernel,
        grid=(4,),
        in_specs=[pl.BlockSpec((part, width), lambda q: (q, 0))] * 3,
        out_specs=[pl.BlockSpec((2, 3, part, cc), lambda q: (q, 0, 0, 0))] * CHUNKS,
        out_shape=[jax.ShapeDtypeStruct((8, 3, part, cc), BF16)] * CHUNKS,
        compiler_params=PARAMS,
        cost_estimate=SMALL,
        name="spread_states",
    )(*arrays)


def add_kernel(here_ref, came_ref, out_ref):
    cc = out_ref.shape[2]
    for g in range(2):
        at = slice(g * cc, (g + 1) * cc)
        out_ref[g] = (here_ref[:, at].astype(F32) + came_ref[:, at].astype(F32)).astype(BF16)


def add_halves(here, came):
    rows, cut = came.shape
    part = rows // 4
    return pl.pallas_call(
        add_kernel,
        grid=(4,),
        in_specs=[pl.BlockSpec((part, cut), lambda q: (q, 0))] * 2,
        out_specs=pl.BlockSpec((2, part, cut // 2), lambda q: (q, 0, 0)),
        out_shape=jax.ShapeDtypeStruct((8, part, cut // 2), BF16),
        compiler_params=PARAMS,
        cost_estimate=SMALL,
        name="add_halves",
    )(here, came)


def take_pieces(pool, places):
    number, block = places.shape[0], pool.shape[1:]

    def kernel(places_ref, pool_ref, out_ref, buffers, sems):
        loads = [
            pltpu.make_async_copy(pool_ref.at[places_ref[j]], buffers.at[j], sems.at[0, j])
            for j in range(number)
        ]
        stores = [
            pltpu.make_async_copy(buffers.at[j], out_ref.at[j], sems.at[1, j]) for j in range(number)
        ]
        for load in loads:
            load.start()
        for load, back in zip(loads, stores):
            load.wait()
            back.start()
        for back in stores:
            back.wait()

    return pl.pallas_call(
        kernel,
        in_specs=[pl.BlockSpec(memory_space=pltpu.SMEM), ANYWHERE],
        out_specs=ANYWHERE,
        out_shape=jax.ShapeDtypeStruct((number,) + block, BF16),
        scratch_shapes=[pltpu.VMEM((number,) + block, BF16), pltpu.SemaphoreType.DMA((2, number))],
        compiler_params=PARAMS,
        cost_estimate=SMALL,
        name="take_pieces",
    )(places, pool)


def adam_kernel(table_ref, *refs):
    pools, out_ref = refs[:4], refs[4]
    step = 16

    def run(held_ref, grad_ref):
        for i in range(grad_ref.shape[1] // step):
            at = slice(i * step, (i + 1) * step)
            state = [held_ref[0, k, at, :].astype(F32) for k in range(3)]
            grad = grad_ref[0, at, :].astype(F32)
            new = adam_update(state[0], grad, state[1], state[2], decay_rate)
            for k in range(3):
                out_ref[0, k, at, :] = new[k].astype(BF16)

    far = table_ref[0, pl.program_id(0)]

    @pl.when(far == 0)
    def _():
        run(pools[0], pools[1])

    @pl.when(far == 1)
    def _():
        run(pools[2], pools[3])


def adam_of_sources(table, near, far):
    part, cc = near[1].shape[1:]
    specs = [
        [
            pl.BlockSpec((1, 3, part, cc), lambda m, t, r=r: (t[r, m], 0, 0, 0)),
            pl.BlockSpec((1, part, cc), lambda m, t, r=r: (t[r, m], 0, 0)),
        ]
        for r in (1, 2)
    ]
    return pl.pallas_call(
        adam_kernel,
        grid_spec=pltpu.PrefetchScalarGridSpec(
            num_scalar_prefetch=1,
            grid=(8,),
            in_specs=specs[0] + specs[1],
            out_specs=pl.BlockSpec((1, 3, part, cc), lambda m, t: (m, 0, 0, 0)),
        ),
        out_shape=jax.ShapeDtypeStruct((8, 3, part, cc), BF16),
        compiler_params=PARAMS,
        cost_estimate=SMALL,
        name="adam_of_sources",
    )(table, *near, *far)


def crossing(source):
    eight = jnp.arange(8, dtype=jnp.int32)
    src = source.reshape(4, 2, 2).transpose(1, 0, 2).reshape(2, 8)
    cross = (src // 2) % 2 != jnp.arange(2, dtype=jnp.int32)[:, None]
    same = src[:, :, None] == src[:, None, :]
    first_same = jnp.min(jnp.where(same, eight[None, None, :], 8), axis=2)
    is_first = cross & (first_same == eight[None, :])
    before = (eight[None, :] < eight[:, None]).astype(jnp.int32)
    rank = jnp.sum(is_first[:, None, :].astype(jnp.int32) * before[None], axis=2)
    slot = jnp.sum(jnp.where(first_same[:, :, None] == eight, rank[:, None, :], 0), axis=2)
    count = jnp.max(jnp.sum(is_first.astype(jnp.int32), axis=1))
    holds = is_first[:, :, None] & (rank[:, :, None] == eight)
    slot_src = jnp.sum(jnp.where(holds, src[:, :, None], 0), axis=1)
    return src, cross.astype(jnp.int32), slot, slot_src, count


def store_kernel(*refs):
    back_ref, outs = refs[0], refs[-3:]
    cc = back_ref.shape[3]
    for g in range(2):
        for k in range(3):
            outs[k][:, g * cc : (g + 1) * cc] = back_ref[g, k]


def store(outs, back, chunk):
    part, cc = back.shape[2:]
    out_spec = pl.BlockSpec((part, 2 * cc), lambda q: (q, chunk))
    return pl.pallas_call(
        store_kernel,
        grid=(4,),
        in_specs=[pl.BlockSpec((2, 3, part, cc), lambda q: (q, 0, 0, 0))] + [ANYWHERE] * len(outs),
        out_specs=[out_spec] * 3,
        out_shape=[jax.ShapeDtypeStruct((4 * part, 2 * cc * CHUNKS), BF16)] * 3,
        input_output_aliases={1 + k: k for k in range(len(outs))},
        compiler_params=STORE_PARAMS,
        cost_estimate=SMALL,
        name="store",
    )(back, *outs)


def gather_rows(w_ref, own_ref, other_ref):
    rows = own_ref.shape[0]

    @pl.when(pl.program_id(0) == 0)
    def _():
        w_ref[:rows] = own_ref[...]
        w_ref[rows:] = other_ref[...]


def input_grad_kernel(y_ref, *refs):
    *ins, w_ref = refs
    cots, (own_ref, other_ref, x_ref), outs, gain_ref = ins[:-8], ins[-8:-5], ins[-5:-1], ins[-1]
    gather_rows(w_ref, own_ref, other_ref)
    turn = pl.program_id(0)
    total = None
    cut = cots[0].shape[1]
    for i, cot in enumerate(cots):
        term = lax.dot_general(
            cot[...],
            w_ref[:, i * cut : (i + 1) * cut],
            (((1,), (1,)), ((), ())),
            preferred_element_type=F32,
        )
        total = term if total is None else total + term

    for d in range(4):

        @pl.when(turn == d)
        def _():
            outs[d][...] = total.astype(BF16)

    @pl.when(turn == 0)
    def _():
        gain_ref[...] = jnp.zeros_like(gain_ref)

    gain_ref[...] += jnp.sum(total * x_ref[...].astype(F32), axis=0, keepdims=True)


def input_grads(cots, w, x, y):
    count, depth = x.shape
    step = count // 4
    row = lambda i, y_ref: ((y_ref[0] + i) % 4, 0)
    whole = lambda i, y_ref: (0, 0)
    *grads, gain = pl.pallas_call(
        input_grad_kernel,
        grid_spec=pltpu.PrefetchScalarGridSpec(
            num_scalar_prefetch=1,
            grid=(4,),
            in_specs=[pl.BlockSpec((step, c.shape[1]), row) for c in cots]
            + [pl.BlockSpec(half.shape, whole) for half in w]
            + [pl.BlockSpec((step, depth), row)],
            out_specs=[pl.BlockSpec((step, depth), whole)] * 4 + [pl.BlockSpec((1, depth), whole)],
            scratch_shapes=[pltpu.VMEM((depth, w[0].shape[1]), BF16)],
        ),
        out_shape=[jax.ShapeDtypeStruct((step, depth), BF16)] * 4
        + [jax.ShapeDtypeStruct((1, depth), F32)],
        compiler_params=PARAMS,
        cost_estimate=SMALL,
        name="input_grads",
    )(y[None], *cots, *w, x)
    return grads, gain


def value_kernel(y_ref, x_ref, w_own_ref, w_other_ref, *refs):
    *outs, w_ref = refs
    gather_rows(w_ref, w_own_ref, w_other_ref)
    turn = pl.program_id(0)
    part = jnp.dot(x_ref[...], w_ref[...], preferred_element_type=F32).astype(BF16)
    half = part.shape[1] // 2
    for d, out in ((0, outs[0]), (1, outs[1]), (3, outs[4])):

        @pl.when(turn == d)
        def _():
            out[...] = part

    @pl.when(turn == 2)
    def _():
        outs[2][...] = part[:, :half]
        outs[3][...] = part[:, half:]


def value_parts(x, w, y):
    count, depth = x.shape
    width = w[0].shape[1]
    step = count // 4
    whole = lambda i, y_ref: (0, 0)
    widths = [width, width, width // 2, width // 2, width]
    return pl.pallas_call(
        value_kernel,
        grid_spec=pltpu.PrefetchScalarGridSpec(
            num_scalar_prefetch=1,
            grid=(4,),
            in_specs=[pl.BlockSpec((step, depth), lambda i, y_ref: ((y_ref[0] + i) % 4, 0))]
            + [pl.BlockSpec(half.shape, whole) for half in w],
            out_specs=[pl.BlockSpec((step, n), whole) for n in widths],
            scratch_shapes=[pltpu.VMEM((depth, width), BF16)],
        ),
        out_shape=[jax.ShapeDtypeStruct((step, n), BF16) for n in widths],
        compiler_params=PARAMS,
        cost_estimate=SMALL,
        name="value_parts",
    )(y[None], x, *w)


def shards(
    hidden,
    value_grad,
    weight,
    moment_one,
    moment_two,
    norm_gain,
    gain_first,
    gain_second,
    donors,
    recipient,
):
    member = lax.axis_index("member")
    fsdp = lax.axis_index("fsdp")
    z, xl, core = member // 4, (member // 2) % 2, member % 2
    xh, y = fsdp // 4, fsdp % 4
    y_at = [(y + d) % 4 for d in range(4)]
    y_from = [(y - d) % 4 for d in range(4)]

    tokens, features = hidden.shape[1:]
    width = value_grad.shape[2]
    rows = features // 8
    cut = width // CHUNKS

    source = jnp.where(recipient == 1, donors, jnp.arange(16, dtype=jnp.int32))
    src, cross, slot, slot_src, count = crossing(source)
    place = lambda s: s // 4 * 2 + s % 2
    my_src, my_cross, my_slot = pick(src, xl), pick(cross, xl), pick(slot, xl)
    leaving = place(pick(slot_src, 1 - xl))
    table = jnp.stack([my_cross, place(my_src), my_slot])
    table_few = jnp.stack([my_cross, place(my_src), jnp.minimum(my_slot, SLOTS - 1)])

    blocks = split_inputs(hidden[0], norm_gain, xh)
    pieces = [pick(blocks, y_at[d]) for d in (1, 2, 3)]
    arrived = [to_fsdp(piece, dy=d) for d, piece in zip((1, 2, 3), pieces)]
    w_quarter = [weight[0], to_fsdp(weight[0], dx=1)]

    cots = [
        lax.all_gather(
            value_grad[0, :, i * cut : (i + 1) * cut], "fsdp", axis_index_groups=Y_GROUPS, tiled=True
        )
        for i in range(CHUNKS)
    ]

    spread = spread_states([tie(weight[0], pieces), moment_one[0], moment_two[0]])
    held0 = swap_members(spread[0])
    sent = take_pieces(held0, leaving[:SLOTS])
    far_held0 = to_member(sent, dx=1)
    held1 = swap_members(tie(spread[1], sent))
    arrived, inputs, _ = lax.optimization_barrier((arrived, blocks, sent))
    for d in (1, 2, 3):
        inputs = put(inputs, arrived[d - 1], y_from[d])
    inputs = inputs.reshape(4 * tokens, 2 * rows)

    partial0 = matmul(inputs, cots[0], (0, 0)).astype(BF16)

    value_part = value_parts(tie(inputs, partial0), w_quarter, y)

    came0 = tie(to_fsdp(partial0[rows:], dx=1), held1, far_held0, value_part[0])
    sum0 = add_halves(partial0, came0)
    grad0 = swap_members(sum0)
    cots[1] = tie(cots[1], sum0)
    partial1 = matmul(inputs, cots[1], (0, 0)).astype(BF16)

    def many(near, far):
        rest = leaving[SLOTS:]
        more = [to_member(take_pieces(pool, rest), dx=1) for pool in near]
        far = [jnp.concatenate(pair) for pair in zip(far, more)]
        return adam_of_sources(table, near, far)

    def new_states(near, far):
        return lax.cond(
            count > SLOTS, many, lambda near, far: adam_of_sources(table_few, near, far), near, far
        )

    grad0 = tie(grad0, partial1)
    sent = take_pieces(grad0, leaving[:SLOTS])
    far_grad0 = to_member(sent, dx=1)

    input_grad, gain_part = input_grads(cots, w_quarter, tie(inputs, partial1), y)
    value_got = {1: to_fsdp(value_part[1], dy=1), 3: to_fsdp(value_part[4], dy=3)}
    value_got[2] = [to_fsdp(half, dy=2) for half in value_part[2:4]]

    came1 = to_fsdp(partial1[rows:], dx=1)
    came1 = tie(came1, input_grad[0], sent, value_got[1], value_got[3])
    sum1 = add_halves(partial1, came1)
    new0 = new_states([held0, grad0], [far_held0, tie(far_grad0, sum1)])
    grad1 = tie(swap_members(sum1), new0)
    far_held1 = to_member(take_pieces(tie(held1, new0), leaving[:SLOTS]), dx=1)
    back0 = swap_members(tie(new0, grad1, value_got[2][0]))
    sent = take_pieces(grad1, leaving[:SLOTS])
    far_grad1 = tie(to_member(sent, dx=1), value_got[2][1])
    new1 = new_states([held1, grad1], [far_held1, far_grad1])
    back1 = swap_members(new1)

    gain_part = tie(gain_part, sent).reshape(2, rows)
    gain_parts = jnp.zeros((4, 2, rows), F32)
    for d in range(4):
        got = to_fsdp(gain_part, dy=d) if d else gain_part
        gain_parts = put(gain_parts, got, y_from[d])
    grads_got = [to_fsdp(input_grad[d], dy=d) for d in (1, 2, 3)]
    gain_sum = gain_parts + to_fsdp(gain_parts, dx=1)[:, ::-1]
    gain_sum = jnp.where(xh == 0, gain_sum, gain_sum[:, ::-1]).transpose(1, 0, 2)
    gain_grad = gain_sum.reshape(1, features) / (1.0 + norm_gain)
    gain_new = jnp.concatenate(
        adam_update(norm_gain, gain_grad, gain_first, gain_second, 0.0)
    )
    gain_every = lax.all_gather(jnp.pad(gain_new, ((0, 2), (0, 0))), "member")
    gain_all = pick(gain_every, pick(source, member))[:3, None]

    outs = store(store([], back0, 0), back1, 1)

    parts = [input_grad[0]] + grads_got
    value_parts_got = [value_part[0], value_got[1], value_got[3], *value_got[2]]
    hidden_grad, values = join_parts(
        hidden[0], tie(norm_gain, new1), parts, value_parts_got, xh, y
    )
    return (
        values[None],
        hidden_grad[None],
        *(out[None] for out in outs),
        gain_all[0],
        gain_all[1],
        gain_all[2],
    )


def solution(mesh):
    tok = P("member", "fsdp", None)
    mem = P("member", None)
    return jax.shard_map(
        shards,
        mesh=mesh,
        in_specs=(tok,) * 5 + (mem,) * 3 + (P(), P()),
        out_specs=(tok,) * 5 + (mem,) * 3,
        check_vma=False,
    )
```

time: 628 us -> 311 us (0.50); the launches traced: 618 us -> 309 us
  waiting for transfers between devices: 256 us -> 107 us
  local copies, waits for them, and re-layouts: 118 us -> 19 us
  blocking collectives: 92.2 us -> 0 us
  Pallas kernels: 0 us -> 83.7 us
  other arithmetic: 65.1 us -> 2.81 us
  starting transfers between devices: 31.7 us -> 67.9 us
  matrix products: 40.3 us -> 11.8 us
    reduce_scatter x1 -> x0, waiting for transfers between devices: 171 us -> none  [shards(): lax.psum_scatter(lax.dot_general(inputs, cotangent, (((0,), (0,)), ((), (...]
    pallas_call x0 -> x15, Pallas kernels: none -> 83.7 us  [the longest x2 14.9 us: adam_of_sources(): pl.pallas_call(adam_kernel, grid_spec=pltpu.PrefetchScalarGridSpec(num_sc...]
    all_gather x3 -> x0, blocking collectives: 61.8 us -> none  [the longest x1 26.1 us: shards(): lax.all_gather(new_second[None], 'member', axis=0, tiled=True)]
    unnamed x35 -> x20, local copies, waits for them, and re-layouts: 63.7 us -> 2.48 us
    ppermute x0 -> x21, waiting for transfers between devices: none -> 60.7 us  [the longest x17 37.9 us: to_fsdp(): return lax.ppermute(x, 'fsdp', pairs)]
    unnamed x4 -> x1, other arithmetic: 47.2 us -> 0.7 us
    all_gather x1 -> x3, waiting for transfers between devices: 32.4 us -> 0.02 us  [the longest x1 0.02 us: shards(): gain_every = lax.all_gather(jnp.pad(gain_new, ((0, 2), (0, 0))), 'member')]
    psum x1 -> x0, blocking collectives: 30.4 us -> none  [shards(): gain_grad = lax.psum(jnp.sum(input_grad * normed, axis=0), 'fsdp')]
  transfers between devices with their start and end apart: 8 -> 30, of which waited for: 6 -> 13; matrix products, arithmetic and copies ran while one was open for 33% -> 9% of each run, Pallas kernels for 0% -> 25%
where the time goes in v1:
time: 311 us; the launch traced here: 309 us
  waiting for transfers between devices  107 us (34%)
  Pallas kernels  83.7 us (27%)
  starting transfers between devices  67.9 us (22%)
  local copies, waits for them, and re-layouts  19 us (6%)
  between operations  16.8 us (5%)
  matrix products  11.8 us (4%)
    all_to_all x6, waiting for transfers between devices, swap_members(): return lax.all_to_all(x, 'member', 0, 0, axis_index_groups=X_GROUPS)  45.7 us
    all_to_all x6, starting transfers between devices, swap_members(): return lax.all_to_all(x, 'member', 0, 0, axis_index_groups=X_GROUPS)  39.3 us
    ppermute x17, waiting for transfers between devices, to_fsdp(): return lax.ppermute(x, 'fsdp', pairs)  37.9 us
    ppermute x17, starting transfers between devices, to_fsdp(): return lax.ppermute(x, 'fsdp', pairs)  25.5 us
    ppermute x4, waiting for transfers between devices, to_member(): return lax.ppermute(x, 'member', pairs)  22.8 us
    pallas_call x2, Pallas kernels, adam_of_sources(): pl.pallas_call(adam_kernel, grid_spec=pltpu.PrefetchScalarGridSpec(num_sc...  14.9 us
    pallas_call x1, Pallas kernels, input_grads(): pl.pallas_call(input_grad_kernel, grid_spec=pltpu.PrefetchScalarGridSpec(...  13.4 us
    pallas_call x1, Pallas kernels, value_parts(): pl.pallas_call(value_kernel, grid_spec=pltpu.PrefetchScalarGridSpec(num_s...  13.1 us
  transfers between devices with their start and end apart: 30, of which 13 were waited for; matrix products, arithmetic and copies ran while one was open for 9% of the time, Pallas kernels for 25%

profile of v1, /device:TPU:1, one launch (start us, length us, event | category | flops | bytes accessed | tf_op | source)
XLA Modules:
  0.0 309.1 jit_solution(6477419739683664455)
XLA Ops:
  10.0 4.8 %split_inputs.1 = bf16[4,384,896]{2,1,0:T(8,128)(2,1)} custom-call(s32[1]{0:T(128)} %bitcast.xh_ref, bf16[384,3584]{1,0:T(8,128)(2,1)} %bitcast.63, f32[1,3584]{1,0:T(1,128)} %gain_ref.2), custom_call_target="tpu_custom_call" | custom-call | bytes 65536 | tf_op jit(solution)/shard_map/split_inputs/pallas_call | solution.py:92
  14.7 2.8 dynamic-slice_bitcast_fusion
  17.5 5.5 %spread_states.1 = (bf16[8,3,112,512]{3,2,1,0:T(8,128)(2,1)}, bf16[8,3,112,512]{3,2,1,0:T(8,128)(2,1)}) custom-call(bf16[448,2048]{1,0:T(8,128)(2,1)} %bitcast.56, bf16[448,2048]{1,0:T(8,128)(2,1)} %bitcast.65, bf16[448,2048]{1,0:T(8,128)(2,1)} %bitcast.66), custom_call_target="tpu_custom_call" | custom-call | bytes 65536 | tf_op jit(solution)/shard_map/spread_states/pallas_call | solution.py:184
  23.0 7.1 %all-to-all-start = ((bf16[8,3,112,512]{3,2,1,0:T(8,128)(2,1)}), bf16[8,3,112,512]{3,2,1,0:T(8,128)(2,1)S(1)}, u32[]{:S(2)}, u32[]{:S(2)}) async-start(bf16[8,3,112,512]{3,2,1,0:T(8,128)(2,1)} %get-tuple-element.121), calls=%async_computation | async-start | bytes 5505024 | tf_op jit(solution)/shard_map/all_to_all | solution.py:51
  30.8 2.8 collective-permute-start.9
  33.6 2.8 collective-permute-start.6
  38.3 25.2 %all-to-all-done.pool_ref = bf16[8,3,112,512]{3,2,1,0:T(8,128)(2,1)S(1)} async-done(((bf16[8,3,112,512]{3,2,1,0:T(8,128)(2,1)}), bf16[8,3,112,512]{3,2,1,0:T(8,128)(2,1)S(1)}, u32[]{:S(2)}, u32[]{:S(2)}) %all-to-all-start) | async-done | bytes 2752544 | tf_op jit(solution)/shard_map/all_to_all | solution.py:51
  67.7 14.5 %collective-permute-done.4 = bf16[384,896]{1,0:T(8,128)(2,1)} collective-permute-done((bf16[384,896]{1,0:T(8,128)(2,1)S(1)}, bf16[384,896]{1,0:T(8,128)(2,1)}, u32[]{:S(2)}, u32[]{:S(2)}) %collective-permute-start.4) | collective-permute-done | bytes 688160 | tf_op jit(solution)/shard_map/ppermute | solution.py:40
  82.2 5.1 %all-to-all-start.1 = ((bf16[8,3,112,512]{3,2,1,0:T(8,128)(2,1)}), bf16[8,3,112,512]{3,2,1,0:T(8,128)(2,1)}, u32[]{:S(2)}, u32[]{:S(2)}) async-start(bf16[8,3,112,512]{3,2,1,0:T(8,128)(2,1)} %get-tuple-element.122), calls=%async_computation.1 | async-start | bytes 5505024 | tf_op jit(solution)/shard_map/all_to_all | solution.py:51
  93.4 6.0 %convolution_convert_fusion.1.here_ref = bf16[896,1024]{1,0:T(8,128)(2,1)S(1)} fusion(bf16[1536,896]{1,0:T(8,128)(2,1)} %bitcast.52, bf16[1,1536,1024]{2,1,0:T(8,128)(2,1)} %all-gather.10.cloned.1.call-done), kind=kOutput, calls=%fused_computation.5 | convolution fusion | flops 2819489792 | bytes 7733248 | tf_op jit(solution)/shard_map/dot_general | solution.py:67
  104.4 13.1 %value_parts.1 = (bf16[384,2048]{1,0:T(8,128)(2,1)}, bf16[384,2048]{1,0:T(8,128)(2,1)}, bf16[384,1024]{1,0:T(8,128)(2,1)}, bf16[384,1024]{1,0:T(8,128)(2,1)}, bf16[384,2048]{1,0:T(8,128)(2,1)}) custom-call(s32[1]{0:T(128)} %bitcast.1.y_ref, bf16[1536,896]{1,0:T(8,128)(2,1)} %bitcast.53, bf16[448,2048]{1,0:T(8,128)(2,1)} %bitcast.58, ...), custom_call_target="tpu_custom_call" | custom-call | bytes 65536 | tf_op jit(solution)/shard_map/value_parts/pallas_call | solution.py:424
  120.8 4.6 %collective-permute-done.7.came_ref = bf16[448,1024]{1,0:T(8,128)(2,1)} collective-permute-done((bf16[448,1024]{1,0:T(8,128)(2,1)}, bf16[448,1024]{1,0:T(8,128)(2,1)}, u32[]{:S(2)}, u32[]{:S(2)}) %collective-permute-start.7) | collective-permute-done | bytes 917536 | tf_op jit(solution)/shard_map/ppermute | solution.py:40
  125.4 3.6 %add_halves.2 = bf16[8,112,512]{2,1,0:T(8,128)(2,1)} custom-call(bf16[896,1024]{1,0:T(8,128)(2,1)} %copy-done.1, bf16[448,1024]{1,0:T(8,128)(2,1)} %collective-permute-done.7.came_ref), custom_call_target="tpu_custom_call" | custom-call | bytes 65536 | tf_op jit(solution)/shard_map/add_halves/pallas_call | solution.py:206
  129.0 5.8 %convolution_convert_fusion.here_ref = bf16[896,1024]{1,0:T(8,128)(2,1)S(1)} fusion(bf16[1536,896]{1,0:T(8,128)(2,1)} %bitcast.54, bf16[1536,1024]{1,0:T(8,128)(2,1)} %bitcast.61), kind=kOutput, calls=%fused_computation.4 | convolution fusion | flops 2819489792 | bytes 7733248 | tf_op jit(solution)/shard_map/dot_general | solution.py:67
  139.8 5.6 %all-to-all-start.2 = ((bf16[8,112,512]{2,1,0:T(8,128)(2,1)}), bf16[8,112,512]{2,1,0:T(8,128)(2,1)}, u32[]{:S(2)}, u32[]{:S(2)}) async-start(bf16[8,112,512]{2,1,0:T(8,128)(2,1)} %add_halves.2), calls=%async_computation.2 | async-start | bytes 1835008 | tf_op jit(solution)/shard_map/all_to_all | solution.py:51
  145.3 13.4 %input_grads.1 = (bf16[384,896]{1,0:T(8,128)(2,1)}, bf16[384,896]{1,0:T(8,128)(2,1)}, bf16[384,896]{1,0:T(8,128)(2,1)}, bf16[384,896]{1,0:T(8,128)(2,1)}, f32[1,896]{1,0:T(1,128)}) custom-call(s32[1]{0:T(128)} %bitcast.1.y_ref, bf16[1536,1024]{1,0:T(8,128)(2,1)} %bitcast.60, bf16[1536,1024]{1,0:T(8,128)(2,1)} %bitcast.62, bf16[448,2048]{1,0:T(8,128)(2,1)} %bitcast.59, ...), custom_call_target="tpu_custom_call" | custom-call | bytes 65536 | tf_op jit(solution)/shard_map/input_grads/pallas_call | solution.py:380
  161.4 3.7 %add_halves.3 = bf16[8,112,512]{2,1,0:T(8,128)(2,1)} custom-call(bf16[896,1024]{1,0:T(8,128)(2,1)} %copy-done, bf16[448,1024]{1,0:T(8,128)(2,1)} %collective-permute-done.10.came_ref), custom_call_target="tpu_custom_call" | custom-call | bytes 65536 | tf_op jit(solution)/shard_map/add_halves/pallas_call | solution.py:206
  165.1 5.0 %all-to-all-start.3 = ((bf16[8,112,512]{2,1,0:T(8,128)(2,1)}), bf16[8,112,512]{2,1,0:T(8,128)(2,1)}, u32[]{:S(2)}, u32[]{:S(2)}) async-start(bf16[8,112,512]{2,1,0:T(8,128)(2,1)} %add_halves.3), calls=%async_computation.3 | async-start | bytes 1835008 | tf_op jit(solution)/shard_map/all_to_all | solution.py:51
  173.0 7.2 %collective-permute-done.13 = bf16[3,112,512]{2,1,0:T(8,128)(2,1)S(1)} collective-permute-done((bf16[3,112,512]{2,1,0:T(8,128)(2,1)S(1)}, bf16[3,112,512]{2,1,0:T(8,128)(2,1)S(1)}, u32[]{:S(2)}, u32[]{:S(2)}) %collective-permute-start.13) | collective-permute-done | bytes 344096 | tf_op jit(solution)/shard_map/ppermute | solution.py:47
  180.2 7.1 %conditional.2 = (bf16[8,3,112,512]{3,2,1,0:T(8,128)(2,1)}) conditional(s32[]{:T(128)} %convert_element_type.35, (s32[3,8]{1,0:T(4,128)S(1)}, bf16[8,3,112,512]{3,2,1,0:T(8,128)(2,1)S(1)}, bf16[8,112,512]{2,1,0:T(8,128)(2,1)}, bf16[3,3,112,512]{3,2,1,0:T(8,128)(2,1)}, bf16[3,112,512]{2,1,0:T(8,128)(2,1)S(1)}) %tuple.46, (s32[8]{0:T(128)S(1)}, ...), branch_computations={%region_6.7_spmd, %region_7.8_spmd} | conditional | flops 1835008 | bytes 16711808 | solution.py:512
  180.2 7.1 %adam_of_sources.4 = bf16[8,3,112,512]{3,2,1,0:T(8,128)(2,1)} custom-call(s32[3,8]{1,0:T(4,128)S(1)} %get-tuple-element.26.table_ref, bf16[8,3,112,512]{3,2,1,0:T(8,128)(2,1)S(1)} %get-tuple-element.44.refs_0_, bf16[8,112,512]{2,1,0:T(8,128)(2,1)} %get-tuple-element.52.refs_1_, bf16[3,3,112,512]{3,2,1,0:T(8,128)(2,1)} %get-tuple-element.53.refs_2_, ...), custom_call_target="tpu_custom_call" | custom-call | bytes 65536 | tf_op jit(solution)/shard_map/cond/branch_0_fun/adam_of_sources/pallas_call | solution.py:282
  187.3 3.5 %collective-permute-done.20.refs_7_ = bf16[384,1024]{1,0:T(8,128)(2,1)} collective-permute-done((bf16[384,1024]{1,0:T(8,128)(2,1)}, bf16[384,1024]{1,0:T(8,128)(2,1)}, u32[]{:S(2)}, u32[]{:S(2)}) %collective-permute-start.20) | collective-permute-done | bytes 786464 | tf_op jit(solution)/shard_map/ppermute | solution.py:40
  190.8 5.5 %all-to-all-start.5 = ((bf16[8,3,112,512]{3,2,1,0:T(8,128)(2,1)}), bf16[8,3,112,512]{3,2,1,0:T(8,128)(2,1)S(1)}, u32[]{:S(2)}, u32[]{:S(2)}) async-start(bf16[8,3,112,512]{3,2,1,0:T(8,128)(2,1)} %get-tuple-element.181), calls=%async_computation.5 | async-start | bytes 5505024 | tf_op jit(solution)/shard_map/all_to_all | solution.py:51
  201.8 2.9 collective-permute-done.22
  216.6 10.5 %collective-permute-done.16.refs_8_ = bf16[384,1024]{1,0:T(8,128)(2,1)} collective-permute-done((bf16[384,1024]{1,0:T(8,128)(2,1)}, bf16[384,1024]{1,0:T(8,128)(2,1)}, u32[]{:S(2)}, u32[]{:S(2)}) %collective-permute-start.16) | collective-permute-done | bytes 786464 | tf_op jit(solution)/shard_map/ppermute | solution.py:40
  230.7 15.6 %collective-permute-done.15 = bf16[3,112,512]{2,1,0:T(8,128)(2,1)S(1)} collective-permute-done((bf16[3,112,512]{2,1,0:T(8,128)(2,1)S(1)}, bf16[3,112,512]{2,1,0:T(8,128)(2,1)S(1)}, u32[]{:S(2)}, u32[]{:S(2)}) %collective-permute-start.15) | collective-permute-done | bytes 344096 | tf_op jit(solution)/shard_map/ppermute | solution.py:47
  246.3 7.7 %conditional.3 = (bf16[8,3,112,512]{3,2,1,0:T(8,128)(2,1)}) conditional(s32[]{:T(128)} %convert_element_type.35, (s32[3,8]{1,0:T(4,128)S(1)}, bf16[8,3,112,512]{3,2,1,0:T(8,128)(2,1)}, bf16[8,112,512]{2,1,0:T(8,128)(2,1)}, bf16[3,3,112,512]{3,2,1,0:T(8,128)(2,1)}, bf16[3,112,512]{2,1,0:T(8,128)(2,1)S(1)}) %tuple.51, (s32[8]{0:T(128)S(1)}, ...), branch_computations={%region_8.9_spmd, %region_9.10_spmd} | conditional | flops 1835008 | bytes 16711808 | solution.py:512
  246.3 7.7 %adam_of_sources.6 = bf16[8,3,112,512]{3,2,1,0:T(8,128)(2,1)} custom-call(s32[3,8]{1,0:T(4,128)S(1)} %get-tuple-element.61.table_ref, bf16[8,3,112,512]{3,2,1,0:T(8,128)(2,1)} %get-tuple-element.62.refs_0_, bf16[8,112,512]{2,1,0:T(8,128)(2,1)} %get-tuple-element.63.refs_1_, bf16[3,3,112,512]{3,2,1,0:T(8,128)(2,1)} %get-tuple-element.64.refs_2_, ...), custom_call_target="tpu_custom_call" | custom-call | bytes 65536 | tf_op jit(solution)/shard_map/cond/branch_0_fun/adam_of_sources/pallas_call | solution.py:282
  254.0 11.1 %all-to-all-start.4 = ((bf16[8,3,112,512]{3,2,1,0:T(8,128)(2,1)}), bf16[8,3,112,512]{3,2,1,0:T(8,128)(2,1)}, u32[]{:S(2)}, u32[]{:S(2)}) async-start(bf16[8,3,112,512]{3,2,1,0:T(8,128)(2,1)} %get-tuple-element.182), calls=%async_computation.4 | async-start | bytes 5505024 | tf_op jit(solution)/shard_map/all_to_all | solution.py:51
  265.7 9.7 %join_parts.1 = (bf16[384,3584]{1,0:T(8,128)(2,1)}, bf16[384,2048]{1,0:T(8,128)(2,1)}) custom-call(s32[2]{0:T(128)} %pad_add_fusion.3.place_ref, bf16[384,3584]{1,0:T(8,128)(2,1)} %bitcast.64, f32[1,3584]{1,0:T(1,128)} %gain_ref.2, bf16[384,896]{1,0:T(8,128)(2,1)} %get-tuple-element.132.refs_0_, bf16[384,896]{1,0:T(8,128)(2,1)} %collective-permute-done.17.refs_1_, ...), custom_call_target="tpu_custom_call" | custom-call | flops 20000000000 | bytes 10000000 | tf_op jit(solution)/shard_map/join_parts/pallas_call | solution.py:145
  279.1 19.5 %all-to-all-done.4.refs_0_ = bf16[8,3,112,512]{3,2,1,0:T(8,128)(2,1)} async-done(((bf16[8,3,112,512]{3,2,1,0:T(8,128)(2,1)}), bf16[8,3,112,512]{3,2,1,0:T(8,128)(2,1)}, u32[]{:S(2)}, u32[]{:S(2)}) %all-to-all-start.4) | async-done | bytes 2752544 | tf_op jit(solution)/shard_map/all_to_all | solution.py:51
  298.6 4.0 %store.3 = (bf16[448,2048]{1,0:T(8,128)(2,1)}, bf16[448,2048]{1,0:T(8,128)(2,1)}, bf16[448,2048]{1,0:T(8,128)(2,1)}) custom-call(bf16[8,3,112,512]{3,2,1,0:T(8,128)(2,1)} %all-to-all-done.4.refs_0_, bf16[448,2048]{1,0:T(8,128)(2,1)} %get-tuple-element.150.refs_1_, ...), custom_call_target="tpu_custom_call", output_to_operand_aliasing={{0}: (1, {}), {1}: (2, {}), {2}: (3, {})} | custom-call | bytes 65536 | tf_op jit(solution)/shard_map/store/pallas_call | solution.py:324
  (114 shorter events, 56.6 us)
Async XLA Ops:
  7.2 86.2 %all-gather.10.cloned.1.call-start = ((), (), s32[]{:S(2)}) async-start(), calls=%async_computation.7 | async-start | bytes 3932160 | tf_op jit(solution)/shard_map/all_gather | solution.py:479
  23.0 40.5 %all-to-all-start = ((bf16[8,3,112,512]{3,2,1,0:T(8,128)(2,1)}), bf16[8,3,112,512]{3,2,1,0:T(8,128)(2,1)S(1)}, u32[]{:S(2)}, u32[]{:S(2)}) async-start(bf16[8,3,112,512]{3,2,1,0:T(8,128)(2,1)} %get-tuple-element.121), calls=%async_computation | async-start | bytes 5505024 | tf_op jit(solution)/shard_map/all_to_all | solution.py:51
  30.0 99.0 %all-gather.8.cloned.1.call-start = ((), (), s32[]{:S(2)}) async-start(), calls=%async_computation.6 | async-start | bytes 3932160 | tf_op jit(solution)/shard_map/all_gather | solution.py:479
  30.8 73.6 %collective-permute-start.9 = (bf16[448,2048]{1,0:T(8,128)(2,1)}, bf16[448,2048]{1,0:T(8,128)(2,1)}, u32[]{:S(2)}, u32[]{:S(2)}) collective-permute-start(bf16[448,2048]{1,0:T(8,128)(2,1)} %bitcast.57), channel_id=1, source_target_pairs={{0,4},{1,5},{2,6},{3,7},{4,0},{5,1},{6,2},{7,3},{8,12},{9,13},{10,... | collective-permute-start | bytes 5505032 | tf_op jit(solution)/shard_map/ppermute | solution.py:40
  33.6 33.2 %collective-permute-start.6 = (bf16[384,896]{1,0:T(8,128)(2,1)}, bf16[384,896]{1,0:T(8,128)(2,1)}, u32[]{:S(2)}, u32[]{:S(2)}) collective-permute-start(bf16[384,896]{1,0:T(8,128)(2,1)} %get-tuple-element.169), channel_id=1, source_target_pairs={{0,3},{1,0},{2,1},{3,2},{4,7},{5,4},{6,5},{7,6},{8,11},{9,8},{10,9... | collective-permute-start | bytes 2064392 | tf_op jit(solution)/shard_map/ppermute | solution.py:40
  36.4 31.3 %collective-permute-start.5 = (bf16[384,896]{1,0:T(8,128)(2,1)}, bf16[384,896]{1,0:T(8,128)(2,1)}, u32[]{:S(2)}, u32[]{:S(2)}) collective-permute-start(bf16[384,896]{1,0:T(8,128)(2,1)} %get-tuple-element.170), channel_id=1, source_target_pairs={{0,2},{1,3},{2,0},{3,1},{4,6},{5,7},{6,4},{7,5},{8,10},{9,11},{10,... | collective-permute-start | bytes 2064392 | tf_op jit(solution)/shard_map/ppermute | solution.py:40
  36.7 45.5 %collective-permute-start.4 = (bf16[384,896]{1,0:T(8,128)(2,1)S(1)}, bf16[384,896]{1,0:T(8,128)(2,1)}, u32[]{:S(2)}, u32[]{:S(2)}) collective-permute-start(bf16[384,896]{1,0:T(8,128)(2,1)S(1)} %get-tuple-element.171), channel_id=1, source_target_pairs={{0,1},{1,2},{2,3},{3,0},{4,5},{5,6},{6,7},{7,4},{8,9},{9,10},{10,1... | collective-permute-start | bytes 2064392 | tf_op jit(solution)/shard_map/ppermute | solution.py:40
  65.5 54.7 %collective-permute-start.8 = (bf16[3,3,112,512]{3,2,1,0:T(8,128)(2,1)}, bf16[3,3,112,512]{3,2,1,0:T(8,128)(2,1)}, u32[]{:S(2)}, u32[]{:S(2)}) collective-permute-start(bf16[3,3,112,512]{3,2,1,0:T(8,128)(2,1)} %take_pieces.12), channel_id=1, source_target_pairs={{0,16},{8,24},{16,0},{24,8},{32,48},{40,56},{48,32},{56,40},{64,80... | collective-permute-start | bytes 3096584 | tf_op jit(solution)/shard_map/ppermute | solution.py:47
  82.2 38.6 %all-to-all-start.1 = ((bf16[8,3,112,512]{3,2,1,0:T(8,128)(2,1)}), bf16[8,3,112,512]{3,2,1,0:T(8,128)(2,1)}, u32[]{:S(2)}, u32[]{:S(2)}) async-start(bf16[8,3,112,512]{3,2,1,0:T(8,128)(2,1)} %get-tuple-element.122), calls=%async_computation.1 | async-start | bytes 5505024 | tf_op jit(solution)/shard_map/all_to_all | solution.py:51
  101.7 23.7 %collective-permute-start.7 = (bf16[448,1024]{1,0:T(8,128)(2,1)}, bf16[448,1024]{1,0:T(8,128)(2,1)}, u32[]{:S(2)}, u32[]{:S(2)}) collective-permute-start(bf16[448,1024]{1,0:T(8,128)(2,1)} %slice.49), channel_id=1, source_target_pairs={{0,4},{1,5},{2,6},{3,7},{4,0},{5,1},{6,2},{7,3},{8,12},{9,13},{10,... | collective-permute-start | bytes 2752520 | tf_op jit(solution)/shard_map/ppermute | solution.py:40
  117.5 43.9 %collective-permute-start.11 = (bf16[384,2048]{1,0:T(8,128)(2,1)}, bf16[384,2048]{1,0:T(8,128)(2,1)}, u32[]{:S(2)}, u32[]{:S(2)}) collective-permute-start(bf16[384,2048]{1,0:T(8,128)(2,1)} %get-tuple-element.134), channel_id=1, source_target_pairs={{0,1},{1,2},{2,3},{3,0},{4,5},{5,6},{6,7},{7,4},{8,9},{9,10},{10,1... | collective-permute-start | bytes 4718600 | tf_op jit(solution)/shard_map/ppermute | solution.py:40
  118.6 42.8 %collective-permute-start.12 = (bf16[384,2048]{1,0:T(8,128)(2,1)}, bf16[384,2048]{1,0:T(8,128)(2,1)}, u32[]{:S(2)}, u32[]{:S(2)}) collective-permute-start(bf16[384,2048]{1,0:T(8,128)(2,1)} %get-tuple-element.135), channel_id=1, source_target_pairs={{0,3},{1,0},{2,1},{3,2},{4,7},{5,4},{6,5},{7,6},{8,11},{9,8},{10,9... | collective-permute-start | bytes 4718600 | tf_op jit(solution)/shard_map/ppermute | solution.py:40
  137.1 24.4 %collective-permute-start.10 = (bf16[448,1024]{1,0:T(8,128)(2,1)}, bf16[448,1024]{1,0:T(8,128)(2,1)}, u32[]{:S(2)}, u32[]{:S(2)}) collective-permute-start(bf16[448,1024]{1,0:T(8,128)(2,1)} %slice.50), channel_id=1, source_target_pairs={{0,4},{1,5},{2,6},{3,7},{4,0},{5,1},{6,2},{7,3},{8,12},{9,13},{10,... | collective-permute-start | bytes 2752520 | tf_op jit(solution)/shard_map/ppermute | solution.py:40
  139.8 19.4 %all-to-all-start.2 = ((bf16[8,112,512]{2,1,0:T(8,128)(2,1)}), bf16[8,112,512]{2,1,0:T(8,128)(2,1)}, u32[]{:S(2)}, u32[]{:S(2)}) async-start(bf16[8,112,512]{2,1,0:T(8,128)(2,1)} %add_halves.2), calls=%async_computation.2 | async-start | bytes 1835008 | tf_op jit(solution)/shard_map/all_to_all | solution.py:51
  165.1 22.2 %all-to-all-start.3 = ((bf16[8,112,512]{2,1,0:T(8,128)(2,1)}), bf16[8,112,512]{2,1,0:T(8,128)(2,1)}, u32[]{:S(2)}, u32[]{:S(2)}) async-start(bf16[8,112,512]{2,1,0:T(8,128)(2,1)} %add_halves.3), calls=%async_computation.3 | async-start | bytes 1835008 | tf_op jit(solution)/shard_map/all_to_all | solution.py:51
  170.1 20.8 %collective-permute-start.20 = (bf16[384,1024]{1,0:T(8,128)(2,1)}, bf16[384,1024]{1,0:T(8,128)(2,1)}, u32[]{:S(2)}, u32[]{:S(2)}) collective-permute-start(bf16[384,1024]{1,0:T(8,128)(2,1)} %get-tuple-element.146), channel_id=1, source_target_pairs={{0,2},{1,3},{2,0},{3,1},{4,6},{5,7},{6,4},{7,5},{8,10},{9,11},{10,... | collective-permute-start | bytes 2359304 | tf_op jit(solution)/shard_map/ppermute | solution.py:40
  170.9 9.3 %collective-permute-start.13 = (bf16[3,112,512]{2,1,0:T(8,128)(2,1)S(1)}, bf16[3,112,512]{2,1,0:T(8,128)(2,1)S(1)}, u32[]{:S(2)}, u32[]{:S(2)}) collective-permute-start(bf16[3,112,512]{2,1,0:T(8,128)(2,1)S(1)} %copy-done.3), channel_id=1, source_target_pairs={{0,16},{8,24},{16,0},{24,8},{32,48},{40,56},{48,32},{56,40},{64,80... | collective-permute-start | bytes 1032200 | tf_op jit(solution)/shard_map/ppermute | solution.py:47
  190.8 63.2 %all-to-all-start.5 = ((bf16[8,3,112,512]{3,2,1,0:T(8,128)(2,1)}), bf16[8,3,112,512]{3,2,1,0:T(8,128)(2,1)S(1)}, u32[]{:S(2)}, u32[]{:S(2)}) async-start(bf16[8,3,112,512]{3,2,1,0:T(8,128)(2,1)} %get-tuple-element.181), calls=%async_computation.5 | async-start | bytes 5505024 | tf_op jit(solution)/shard_map/all_to_all | solution.py:51
  196.3 20.1 %copy-start.6 = (f32[1,3584]{1,0:T(1,128)S(1)}, f32[1,3584]{1,0:T(1,128)}, u32[]{:S(2)}) copy-start(f32[1,3584]{1,0:T(1,128)} %param.21) | copy-start | bytes 43012
  196.3 79.1 %all-gather.12.cloned.1.call-start = ((), (), s32[]{:S(2)}) async-start(), calls=%async_computation.8 | async-start | bytes 1949696 | tf_op jit(solution)/shard_map/all_gather | solution.py:548
  198.6 28.5 %copy-start.2 = (bf16[3,112,512]{2,1,0:T(8,128)(2,1)S(1)}, bf16[3,112,512]{2,1,0:T(8,128)(2,1)}, u32[]{:S(2)}) copy-start(bf16[3,112,512]{2,1,0:T(8,128)(2,1)} %take_pieces.15) | copy-start | bytes 1032196
  198.8 3.0 collective-permute-start.23
  200.5 4.3 %collective-permute-start.22 = (f32[2,448]{1,0:T(2,128)S(1)}, f32[2,448]{1,0:T(2,128)S(1)}, u32[]{:S(2)}, u32[]{:S(2)}) collective-permute-start(f32[2,448]{1,0:T(2,128)S(1)} %reshape.182), channel_id=1, source_target_pairs={{0,2},{1,3},{2,0},{3,1},{4,6},{5,7},{6,4},{7,5},{8,10},{9,11},{10,... | collective-permute-start | bytes 10760 | tf_op jit(solution)/shard_map/ppermute | solution.py:40
  201.6 4.0 %collective-permute-start.21 = (f32[2,448]{1,0:T(2,128)S(1)}, f32[2,448]{1,0:T(2,128)S(1)}, u32[]{:S(2)}, u32[]{:S(2)}) collective-permute-start(f32[2,448]{1,0:T(2,128)S(1)} %reshape.182), channel_id=1, source_target_pairs={{0,1},{1,2},{2,3},{3,0},{4,5},{5,6},{6,7},{7,4},{8,9},{9,10},{10,1... | collective-permute-start | bytes 10760 | tf_op jit(solution)/shard_map/ppermute | solution.py:40
  205.8 9.7 %collective-permute-start.24 = (f32[4,2,448]{2,0,1:T(4,128)S(1)}, f32[4,2,448]{2,0,1:T(4,128)S(1)}, u32[]{:S(2)}, u32[]{:S(2)}) collective-permute-start(f32[4,2,448]{2,0,1:T(4,128)S(1)} %dynamic_update_slice.29), channel_id=1, source_target_pairs={{0,4},{1,5},{2,6},{3,7},{4,0},{5,1},{6,2},{7,3},{8,12},{9,13},{10,... | collective-permute-start | bytes 43016 | tf_op jit(solution)/shard_map/ppermute | solution.py:40
  207.9 19.2 %collective-permute-start.16 = (bf16[384,1024]{1,0:T(8,128)(2,1)}, bf16[384,1024]{1,0:T(8,128)(2,1)}, u32[]{:S(2)}, u32[]{:S(2)}) collective-permute-start(bf16[384,1024]{1,0:T(8,128)(2,1)} %get-tuple-element.140), channel_id=1, source_target_pairs={{0,2},{1,3},{2,0},{3,1},{4,6},{5,7},{6,4},{7,5},{8,10},{9,11},{10,... | collective-permute-start | bytes 2359304 | tf_op jit(solution)/shard_map/ppermute | solution.py:40
  208.6 57.2 %collective-permute-start.17 = (bf16[384,896]{1,0:T(8,128)(2,1)}, bf16[384,896]{1,0:T(8,128)(2,1)}, u32[]{:S(2)}, u32[]{:S(2)}) collective-permute-start(bf16[384,896]{1,0:T(8,128)(2,1)} %get-tuple-element.143), channel_id=1, source_target_pairs={{0,1},{1,2},{2,3},{3,0},{4,5},{5,6},{6,7},{7,4},{8,9},{9,10},{10,1... | collective-permute-start | bytes 2064392 | tf_op jit(solution)/shard_map/ppermute | solution.py:40
  208.6 57.2 %collective-permute-start.18 = (bf16[384,896]{1,0:T(8,128)(2,1)}, bf16[384,896]{1,0:T(8,128)(2,1)}, u32[]{:S(2)}, u32[]{:S(2)}) collective-permute-start(bf16[384,896]{1,0:T(8,128)(2,1)} %get-tuple-element.144), channel_id=1, source_target_pairs={{0,2},{1,3},{2,0},{3,1},{4,6},{5,7},{6,4},{7,5},{8,10},{9,11},{10,... | collective-permute-start | bytes 2064392 | tf_op jit(solution)/shard_map/ppermute | solution.py:40
  210.9 54.8 %collective-permute-start.19 = (bf16[384,896]{1,0:T(8,128)(2,1)}, bf16[384,896]{1,0:T(8,128)(2,1)}, u32[]{:S(2)}, u32[]{:S(2)}) collective-permute-start(bf16[384,896]{1,0:T(8,128)(2,1)} %get-tuple-element.145), channel_id=1, source_target_pairs={{0,3},{1,0},{2,1},{3,2},{4,7},{5,4},{6,5},{7,6},{8,11},{9,8},{10,9... | collective-permute-start | bytes 2064392 | tf_op jit(solution)/shard_map/ppermute | solution.py:40
  215.5 30.8 %collective-permute-start.14 = (bf16[3,3,112,512]{3,2,1,0:T(8,128)(2,1)}, bf16[3,3,112,512]{3,2,1,0:T(8,128)(2,1)}, u32[]{:S(2)}, u32[]{:S(2)}) collective-permute-start(bf16[3,3,112,512]{3,2,1,0:T(8,128)(2,1)} %take_pieces.14), channel_id=1, source_target_pairs={{0,16},{8,24},{16,0},{24,8},{32,48},{40,56},{48,32},{56,40},{64,80... | collective-permute-start | bytes 3096584 | tf_op jit(solution)/shard_map/ppermute | solution.py:47
  227.1 19.2 %collective-permute-start.15 = (bf16[3,112,512]{2,1,0:T(8,128)(2,1)S(1)}, bf16[3,112,512]{2,1,0:T(8,128)(2,1)S(1)}, u32[]{:S(2)}, u32[]{:S(2)}) collective-permute-start(bf16[3,112,512]{2,1,0:T(8,128)(2,1)S(1)} %copy-done.2), channel_id=1, source_target_pairs={{0,16},{8,24},{16,0},{24,8},{32,48},{40,56},{48,32},{56,40},{64,80... | collective-permute-start | bytes 1032200 | tf_op jit(solution)/shard_map/ppermute | solution.py:47
  254.0 44.6 %all-to-all-start.4 = ((bf16[8,3,112,512]{3,2,1,0:T(8,128)(2,1)}), bf16[8,3,112,512]{3,2,1,0:T(8,128)(2,1)}, u32[]{:S(2)}, u32[]{:S(2)}) async-start(bf16[8,3,112,512]{3,2,1,0:T(8,128)(2,1)} %get-tuple-element.182), calls=%async_computation.4 | async-start | bytes 5505024 | tf_op jit(solution)/shard_map/all_to_all | solution.py:51
  (8 other events, 92.4 us)
Sparse Core Ops, SparseCore 0:
  10.2 69.2 all-gather.9
  81.2 41.3 all-gather.7
  228.3 38.2 all-gather.11

commit v2 on v1

--- a/solution.py
+++ b/solution.py
@@ -246,6 +246,39 @@
     )(places, pool)
 
 
+def put_blocks(blocks, parts, places):
+    number, block = len(parts), parts[0].shape
+
+    def kernel(places_ref, *refs):
+        out_ref, buffers, sems = refs[number + 1 :]
+        loads = [
+            pltpu.make_async_copy(refs[k], buffers.at[k], sems.at[0, k]) for k in range(number)
+        ]
+        stores = [
+            pltpu.make_async_copy(buffers.at[k], out_ref.at[places_ref[k]], sems.at[1, k])
+            for k in range(number)
+        ]
+        for load in loads:
+            load.start()
+        for load, back in zip(loads, stores):
+            load.wait()
+            back.start()
+        for back in stores:
+            back.wait()
+
+    return pl.pallas_call(
+        kernel,
+        in_specs=[pl.BlockSpec(memory_space=pltpu.SMEM)] + [ANYWHERE] * (number + 1),
+        out_specs=ANYWHERE,
+        out_shape=jax.ShapeDtypeStruct(blocks.shape, BF16),
+        input_output_aliases={number + 1: 0},
+        scratch_shapes=[pltpu.VMEM((number,) + block, BF16), pltpu.SemaphoreType.DMA((2, number))],
+        compiler_params=PARAMS,
+        cost_estimate=SMALL,
+        name="put_blocks",
+    )(places, *parts, blocks)
+
+
 def adam_kernel(table_ref, *refs):
     pools, out_ref = refs[:4], refs[4]
     step = 16
@@ -486,19 +519,16 @@
     held0 = swap_members(spread[0])
     sent = take_pieces(held0, leaving[:SLOTS])
     far_held0 = to_member(sent, dx=1)
-    held1 = swap_members(tie(spread[1], sent))
-    arrived, inputs, _ = lax.optimization_barrier((arrived, blocks, sent))
-    for d in (1, 2, 3):
-        inputs = put(inputs, arrived[d - 1], y_from[d])
-    inputs = inputs.reshape(4 * tokens, 2 * rows)
+    arrived, blocks, w_quarter, _ = lax.optimization_barrier((arrived, blocks, w_quarter, sent))
+    inputs = put_blocks(blocks, arrived, jnp.stack(y_from[1:])).reshape(4 * tokens, 2 * rows)
 
     partial0 = matmul(inputs, cots[0], (0, 0)).astype(BF16)
+    held1 = swap_members(tie(spread[1], partial0, far_held0))
 
     value_part = value_parts(tie(inputs, partial0), w_quarter, y)
 
-    came0 = tie(to_fsdp(partial0[rows:], dx=1), held1, far_held0, value_part[0])
+    came0 = tie(to_fsdp(partial0[rows:], dx=1), far_held0, value_part[0])
     sum0 = add_halves(partial0, came0)
-    grad0 = swap_members(sum0)
     cots[1] = tie(cots[1], sum0)
     partial1 = matmul(inputs, cots[1], (0, 0)).astype(BF16)
 
@@ -513,7 +543,7 @@
             count > SLOTS, many, lambda near, far: adam_of_sources(table_few, near, far), near, far
         )
 
-    grad0 = tie(grad0, partial1)
+    grad0 = swap_members(tie(sum0, held1, partial1))
     sent = take_pieces(grad0, leaving[:SLOTS])
     far_grad0 = to_member(sent, dx=1)
 
@@ -529,8 +559,8 @@
     far_held1 = to_member(take_pieces(tie(held1, new0), leaving[:SLOTS]), dx=1)
     back0 = swap_members(tie(new0, grad1, value_got[2][0]))
     sent = take_pieces(grad1, leaving[:SLOTS])
-    far_grad1 = tie(to_member(sent, dx=1), value_got[2][1])
-    new1 = new_states([held1, grad1], [far_held1, far_grad1])
+    far_grad1 = to_member(tie(sent, far_held1), dx=1)
+    new1 = new_states([held1, grad1], [far_held1, tie(far_grad1, value_got[2][1])])
     back1 = swap_members(new1)
 
     gain_part = tie(gain_part, sent).reshape(2, rows)
@@ -538,7 +568,7 @@
     for d in range(4):
         got = to_fsdp(gain_part, dy=d) if d else gain_part
         gain_parts = put(gain_parts, got, y_from[d])
-    grads_got = [to_fsdp(input_grad[d], dy=d) for d in (1, 2, 3)]
+    grads_got = [to_fsdp(tie(input_grad[d], far_grad1), dy=d) for d in (1, 2, 3)]
     gain_sum = gain_parts + to_fsdp(gain_parts, dx=1)[:, ::-1]
     gain_sum = jnp.where(xh == 0, gain_sum, gain_sum[:, ::-1]).transpose(1, 0, 2)
     gain_grad = gain_sum.reshape(1, features) / (1.0 + norm_gain)

time: 311 us -> 299 us (0.961)
  local copies, waits for them, and re-layouts: 19 us -> 12.2 us
  waiting for transfers between devices: 107 us -> 102 us
  starting transfers between devices: 67.9 us -> 63.5 us
    all_to_all x6, waiting for transfers between devices: 45.7 us -> 39.1 us  [swap_members(): return lax.all_to_all(x, 'member', 0, 0, axis_index_groups=X_GROUPS)]
    dynamic_update_slice x7 -> x4, local copies, waits for them, and re-layouts: 6.24 us -> 0.19 us  [put(): return lax.dynamic_update_index_in_dim(x, part, index, axis)]
    ppermute x17, waiting for transfers between devices: 37.9 us -> 43 us  [to_fsdp(): return lax.ppermute(x, 'fsdp', pairs)]
    ppermute x4, waiting for transfers between devices: 22.8 us -> 18.3 us  [to_member(): return lax.ppermute(x, 'member', pairs)]
    pallas_call x0 -> x1, Pallas kernels: none -> 3.11 us  [put_blocks(): pl.pallas_call(kernel, in_specs=[pl.BlockSpec(memory_space=pltpu.SMEM)] +...]
  transfers between devices with their start and end apart: 30 -> 30, of which waited for: 13 -> 15; matrix products, arithmetic and copies ran while one was open for 9% -> 8% of each run, Pallas kernels for 25% -> 27%
where the time goes in v2:
time: 299 us; the launch traced here: 297 us
  waiting for transfers between devices  102 us (34%)
  Pallas kernels  86.5 us (29%)
  starting transfers between devices  63.5 us (21%)
  between operations  16.7 us (6%)
  matrix products  12.8 us (4%)
  local copies, waits for them, and re-layouts  12.2 us (4%)
  other arithmetic  3.41 us (1%)
    ppermute x17, waiting for transfers between devices, to_fsdp(): return lax.ppermute(x, 'fsdp', pairs)  43 us
    all_to_all x6, waiting for transfers between devices, swap_members(): return lax.all_to_all(x, 'member', 0, 0, axis_index_groups=X_GROUPS)  39.1 us
    all_to_all x6, starting transfers between devices, swap_members(): return lax.all_to_all(x, 'member', 0, 0, axis_index_groups=X_GROUPS)  36.8 us
    ppermute x17, starting transfers between devices, to_fsdp(): return lax.ppermute(x, 'fsdp', pairs)  22.8 us
    ppermute x4, waiting for transfers between devices, to_member(): return lax.ppermute(x, 'member', pairs)  18.3 us
    pallas_call x2, Pallas kernels, adam_of_sources(): pl.pallas_call(adam_kernel, grid_spec=pltpu.PrefetchScalarGridSpec(num_sc...  15.2 us
    pallas_call x1, Pallas kernels, input_grads(): pl.pallas_call(input_grad_kernel, grid_spec=pltpu.PrefetchScalarGridSpec(...  13.3 us
    pallas_call x1, Pallas kernels, value_parts(): pl.pallas_call(value_kernel, grid_spec=pltpu.PrefetchScalarGridSpec(num_s...  13.1 us
  transfers between devices with their start and end apart: 30, of which 15 were waited for; matrix products, arithmetic and copies ran while one was open for 8% of the time, Pallas kernels for 27%

profile of v2, /device:TPU:1, one launch (start us, length us, event | category | flops | bytes accessed | tf_op | source)
XLA Modules:
  0.0 296.8 jit_solution(9932807641572079104)
XLA Ops:
  9.9 4.8 %split_inputs.1.refs_3_ = bf16[4,384,896]{2,1,0:T(8,128)(2,1)} custom-call(s32[1]{0:T(128)} %bitcast.xh_ref, bf16[384,3584]{1,0:T(8,128)(2,1)} %bitcast.60, f32[1,3584]{1,0:T(1,128)} %gain_ref.2), custom_call_target="tpu_custom_call" | custom-call | bytes 65536 | tf_op jit(solution)/shard_map/split_inputs/pallas_call | solution.py:92
  17.5 5.4 %spread_states.1 = (bf16[8,3,112,512]{3,2,1,0:T(8,128)(2,1)}, bf16[8,3,112,512]{3,2,1,0:T(8,128)(2,1)}) custom-call(bf16[448,2048]{1,0:T(8,128)(2,1)} %bitcast.53, bf16[448,2048]{1,0:T(8,128)(2,1)} %bitcast.62, bf16[448,2048]{1,0:T(8,128)(2,1)} %bitcast.63), custom_call_target="tpu_custom_call" | custom-call | bytes 65536 | tf_op jit(solution)/shard_map/spread_states/pallas_call | solution.py:184
  22.9 7.1 %all-to-all-start = ((bf16[8,3,112,512]{3,2,1,0:T(8,128)(2,1)}), bf16[8,3,112,512]{3,2,1,0:T(8,128)(2,1)S(1)}, u32[]{:S(2)}, u32[]{:S(2)}) async-start(bf16[8,3,112,512]{3,2,1,0:T(8,128)(2,1)} %get-tuple-element.127), calls=%async_computation | async-start | bytes 5505024 | tf_op jit(solution)/shard_map/all_to_all | solution.py:51
  30.7 2.8 collective-permute-start.7
  38.1 25.3 %all-to-all-done.pool_ref = bf16[8,3,112,512]{3,2,1,0:T(8,128)(2,1)S(1)} async-done(((bf16[8,3,112,512]{3,2,1,0:T(8,128)(2,1)}), bf16[8,3,112,512]{3,2,1,0:T(8,128)(2,1)S(1)}, u32[]{:S(2)}, u32[]{:S(2)}) %all-to-all-start) | async-done | bytes 2752544 | tf_op jit(solution)/shard_map/all_to_all | solution.py:51
  67.7 14.5 %collective-permute-done.4.refs_0_ = bf16[384,896]{1,0:T(8,128)(2,1)} collective-permute-done((bf16[384,896]{1,0:T(8,128)(2,1)S(1)}, bf16[384,896]{1,0:T(8,128)(2,1)}, u32[]{:S(2)}, u32[]{:S(2)}) %collective-permute-start.4) | collective-permute-done | bytes 688160 | tf_op jit(solution)/shard_map/ppermute | solution.py:40
  82.2 3.1 %put_blocks.1 = bf16[4,384,896]{2,1,0:T(8,128)(2,1)} custom-call(s32[3]{0:T(128)} %pad_add_fusion.4.places_ref, bf16[384,896]{1,0:T(8,128)(2,1)} %collective-permute-done.4.refs_0_, bf16[384,896]{1,0:T(8,128)(2,1)} %collective-permute-done.5.refs_1_, bf16[384,896]{1,0:T(8,128)(2,1)} %collective-permute-done.6.refs_2_, ...), custom_call_target="tpu_custom_call", output_to_operand_aliasing={{}: (4, {})} | custom-call | bytes 65536 | tf_op jit(solution)/shard_map/put_blocks/pallas_call | solution.py:269
  85.4 7.0 %convolution_convert_fusion.1.here_ref = bf16[896,1024]{1,0:T(8,128)(2,1)} fusion(bf16[1536,896]{1,0:T(8,128)(2,1)} %bitcast.49, bf16[1,1536,1024]{2,1,0:T(8,128)(2,1)} %all-gather.8.cloned.1.call-done), kind=kOutput, calls=%fused_computation.5 | convolution fusion | flops 2819489792 | bytes 7733248 | tf_op jit(solution)/shard_map/dot_general | solution.py:67
  92.4 4.0 %collective-permute-done.8 = bf16[3,3,112,512]{3,2,1,0:T(8,128)(2,1)} collective-permute-done((bf16[3,3,112,512]{3,2,1,0:T(8,128)(2,1)}, bf16[3,3,112,512]{3,2,1,0:T(8,128)(2,1)}, u32[]{:S(2)}, u32[]{:S(2)}) %collective-permute-start.8) | collective-permute-done | bytes 1032224 | tf_op jit(solution)/shard_map/ppermute | solution.py:47
  96.4 5.2 %all-to-all-start.1 = ((bf16[8,3,112,512]{3,2,1,0:T(8,128)(2,1)}), bf16[8,3,112,512]{3,2,1,0:T(8,128)(2,1)S(1)}, u32[]{:S(2)}, u32[]{:S(2)}) async-start(bf16[8,3,112,512]{3,2,1,0:T(8,128)(2,1)} %get-tuple-element.132), calls=%async_computation.1 | async-start | bytes 5505024 | tf_op jit(solution)/shard_map/all_to_all | solution.py:51
  104.7 13.1 %value_parts.1 = (bf16[384,2048]{1,0:T(8,128)(2,1)}, bf16[384,2048]{1,0:T(8,128)(2,1)}, bf16[384,1024]{1,0:T(8,128)(2,1)}, bf16[384,1024]{1,0:T(8,128)(2,1)}, bf16[384,2048]{1,0:T(8,128)(2,1)}) custom-call(s32[1]{0:T(128)} %bitcast.1.y_ref, bf16[1536,896]{1,0:T(8,128)(2,1)} %bitcast.50, bf16[448,2048]{1,0:T(8,128)(2,1)} %bitcast.55, ...), custom_call_target="tpu_custom_call" | custom-call | bytes 65536 | tf_op jit(solution)/shard_map/value_parts/pallas_call | solution.py:457
  120.7 5.9 %collective-permute-done.9.came_ref = bf16[448,1024]{1,0:T(8,128)(2,1)S(1)} collective-permute-done((bf16[448,1024]{1,0:T(8,128)(2,1)S(1)}, bf16[448,1024]{1,0:T(8,128)(2,1)S(1)}, u32[]{:S(2)}, u32[]{:S(2)}) %collective-permute-start.9) | collective-permute-done | bytes 917536 | tf_op jit(solution)/shard_map/ppermute | solution.py:40
  127.5 3.7 %add_halves.2 = bf16[8,112,512]{2,1,0:T(8,128)(2,1)} custom-call(bf16[896,1024]{1,0:T(8,128)(2,1)} %convolution_convert_fusion.1.here_ref, bf16[448,1024]{1,0:T(8,128)(2,1)} %copy-done.5), custom_call_target="tpu_custom_call" | custom-call | bytes 65536 | tf_op jit(solution)/shard_map/add_halves/pallas_call | solution.py:206
  131.1 5.8 %convolution_convert_fusion.here_ref = bf16[896,1024]{1,0:T(8,128)(2,1)S(1)} fusion(bf16[1536,896]{1,0:T(8,128)(2,1)} %bitcast.51, bf16[1536,1024]{1,0:T(8,128)(2,1)} %bitcast.58), kind=kOutput, calls=%fused_computation.4 | convolution fusion | flops 2819489792 | bytes 7733248 | tf_op jit(solution)/shard_map/dot_general | solution.py:67
  140.2 5.4 %all-to-all-start.2 = ((bf16[8,112,512]{2,1,0:T(8,128)(2,1)}), bf16[8,112,512]{2,1,0:T(8,128)(2,1)}, u32[]{:S(2)}, u32[]{:S(2)}) async-start(bf16[8,112,512]{2,1,0:T(8,128)(2,1)} %add_halves.2), calls=%async_computation.2 | async-start | bytes 1835008 | tf_op jit(solution)/shard_map/all_to_all | solution.py:51
  145.7 13.3 %input_grads.1 = (bf16[384,896]{1,0:T(8,128)(2,1)}, bf16[384,896]{1,0:T(8,128)(2,1)}, bf16[384,896]{1,0:T(8,128)(2,1)}, bf16[384,896]{1,0:T(8,128)(2,1)}, f32[1,896]{1,0:T(1,128)}) custom-call(s32[1]{0:T(128)} %bitcast.1.y_ref, bf16[1536,1024]{1,0:T(8,128)(2,1)} %bitcast.57, bf16[1536,1024]{1,0:T(8,128)(2,1)} %bitcast.59, bf16[448,2048]{1,0:T(8,128)(2,1)} %bitcast.56, ...), custom_call_target="tpu_custom_call" | custom-call | bytes 65536 | tf_op jit(solution)/shard_map/input_grads/pallas_call | solution.py:413
  161.8 3.7 %add_halves.3 = bf16[8,112,512]{2,1,0:T(8,128)(2,1)} custom-call(bf16[896,1024]{1,0:T(8,128)(2,1)} %copy-done.4, bf16[448,1024]{1,0:T(8,128)(2,1)} %collective-permute-done.10.came_ref), custom_call_target="tpu_custom_call" | custom-call | bytes 65536 | tf_op jit(solution)/shard_map/add_halves/pallas_call | solution.py:206
  165.5 5.3 %all-to-all-start.3 = ((bf16[8,112,512]{2,1,0:T(8,128)(2,1)}), bf16[8,112,512]{2,1,0:T(8,128)(2,1)}, u32[]{:S(2)}, u32[]{:S(2)}) async-start(bf16[8,112,512]{2,1,0:T(8,128)(2,1)} %add_halves.3), calls=%async_computation.3 | async-start | bytes 1835008 | tf_op jit(solution)/shard_map/all_to_all | solution.py:51
  170.8 2.9 collective-permute-start.20
  176.5 6.6 %collective-permute-done.13 = bf16[3,112,512]{2,1,0:T(8,128)(2,1)S(1)} collective-permute-done((bf16[3,112,512]{2,1,0:T(8,128)(2,1)S(1)}, bf16[3,112,512]{2,1,0:T(8,128)(2,1)S(1)}, u32[]{:S(2)}, u32[]{:S(2)}) %collective-permute-start.13) | collective-permute-done | bytes 344096 | tf_op jit(solution)/shard_map/ppermute | solution.py:47
  183.1 7.6 %conditional.2 = (bf16[8,3,112,512]{3,2,1,0:T(8,128)(2,1)}) conditional(s32[]{:T(128)} %convert_element_type.35, (s32[3,8]{1,0:T(4,128)S(1)}, bf16[8,3,112,512]{3,2,1,0:T(8,128)(2,1)}, bf16[8,112,512]{2,1,0:T(8,128)(2,1)}, bf16[3,3,112,512]{3,2,1,0:T(8,128)(2,1)}, bf16[3,112,512]{2,1,0:T(8,128)(2,1)S(1)}) %tuple.90, (s32[8]{0:T(128)S(1)}, ...), branch_computations={%region_6.7_spmd, %region_7.8_spmd} | conditional | flops 1835008 | bytes 27721884 | solution.py:542
  183.1 7.6 %adam_of_sources.4 = bf16[8,3,112,512]{3,2,1,0:T(8,128)(2,1)} custom-call(s32[3,8]{1,0:T(4,128)S(1)} %get-tuple-element.26.table_ref, bf16[8,3,112,512]{3,2,1,0:T(8,128)(2,1)} %get-tuple-element.44.refs_0_, bf16[8,112,512]{2,1,0:T(8,128)(2,1)} %get-tuple-element.52.refs_1_, bf16[3,3,112,512]{3,2,1,0:T(8,128)(2,1)} %get-tuple-element.53.refs_2_, ...), custom_call_target="tpu_custom_call" | custom-call | bytes 65536 | tf_op jit(solution)/shard_map/cond/branch_0_fun/adam_of_sources/pallas_call | solution.py:315
  194.0 6.0 %all-to-all-start.5 = ((bf16[8,3,112,512]{3,2,1,0:T(8,128)(2,1)}), bf16[8,3,112,512]{3,2,1,0:T(8,128)(2,1)S(1)}, u32[]{:S(2)}, u32[]{:S(2)}) async-start(bf16[8,3,112,512]{3,2,1,0:T(8,128)(2,1)} %get-tuple-element.193), calls=%async_computation.5 | async-start | bytes 5505024 | tf_op jit(solution)/shard_map/all_to_all | solution.py:51
  210.7 7.0 %collective-permute-done.24 = f32[4,2,448]{2,0,1:T(4,128)S(1)} collective-permute-done((f32[4,2,448]{2,0,1:T(4,128)S(1)}, f32[4,2,448]{2,0,1:T(4,128)S(1)}, u32[]{:S(2)}, u32[]{:S(2)}) %collective-permute-start.24) | collective-permute-done | bytes 14368 | tf_op jit(solution)/shard_map/ppermute | solution.py:40
  218.1 7.7 %collective-permute-done.15 = bf16[3,112,512]{2,1,0:T(8,128)(2,1)S(1)} collective-permute-done((bf16[3,112,512]{2,1,0:T(8,128)(2,1)}, bf16[3,112,512]{2,1,0:T(8,128)(2,1)S(1)}, u32[]{:S(2)}, u32[]{:S(2)}) %collective-permute-start.15) | collective-permute-done | bytes 344096 | tf_op jit(solution)/shard_map/ppermute | solution.py:47
  231.7 7.6 %conditional.3 = (bf16[8,3,112,512]{3,2,1,0:T(8,128)(2,1)}) conditional(s32[]{:T(128)} %convert_element_type.35, (s32[3,8]{1,0:T(4,128)S(1)}, bf16[8,3,112,512]{3,2,1,0:T(8,128)(2,1)}, bf16[8,112,512]{2,1,0:T(8,128)(2,1)}, bf16[3,3,112,512]{3,2,1,0:T(8,128)(2,1)}, bf16[3,112,512]{2,1,0:T(8,128)(2,1)S(1)}) %tuple.88, (s32[8]{0:T(128)S(1)}, ...), branch_computations={%region_8.9_spmd, %region_9.10_spmd} | conditional | flops 1835008 | bytes 27721884 | solution.py:542
  231.7 7.6 %adam_of_sources.6 = bf16[8,3,112,512]{3,2,1,0:T(8,128)(2,1)} custom-call(s32[3,8]{1,0:T(4,128)S(1)} %get-tuple-element.61.table_ref, bf16[8,3,112,512]{3,2,1,0:T(8,128)(2,1)} %get-tuple-element.62.refs_0_, bf16[8,112,512]{2,1,0:T(8,128)(2,1)} %get-tuple-element.63.refs_1_, bf16[3,3,112,512]{3,2,1,0:T(8,128)(2,1)} %get-tuple-element.64.refs_2_, ...), custom_call_target="tpu_custom_call" | custom-call | bytes 65536 | tf_op jit(solution)/shard_map/cond/branch_0_fun/adam_of_sources/pallas_call | solution.py:315
  239.3 7.8 %all-to-all-start.4 = ((bf16[8,3,112,512]{3,2,1,0:T(8,128)(2,1)}), bf16[8,3,112,512]{3,2,1,0:T(8,128)(2,1)}, u32[]{:S(2)}, u32[]{:S(2)}) async-start(bf16[8,3,112,512]{3,2,1,0:T(8,128)(2,1)} %get-tuple-element.194), calls=%async_computation.4 | async-start | bytes 5505024 | tf_op jit(solution)/shard_map/all_to_all | solution.py:51
  247.6 11.3 %collective-permute-done.18.refs_2_ = bf16[384,896]{1,0:T(8,128)(2,1)} collective-permute-done((bf16[384,896]{1,0:T(8,128)(2,1)}, bf16[384,896]{1,0:T(8,128)(2,1)}, u32[]{:S(2)}, u32[]{:S(2)}) %collective-permute-start.18) | collective-permute-done | bytes 688160 | tf_op jit(solution)/shard_map/ppermute | solution.py:40
  258.9 9.7 %join_parts.1 = (bf16[384,3584]{1,0:T(8,128)(2,1)}, bf16[384,2048]{1,0:T(8,128)(2,1)}) custom-call(s32[2]{0:T(128)} %pad_add_fusion.3.place_ref, bf16[384,3584]{1,0:T(8,128)(2,1)} %bitcast.61, f32[1,3584]{1,0:T(1,128)} %gain_ref.2, bf16[384,896]{1,0:T(8,128)(2,1)} %get-tuple-element.140.refs_0_, bf16[384,896]{1,0:T(8,128)(2,1)} %collective-permute-done.17.refs_1_, ...), custom_call_target="tpu_custom_call" | custom-call | flops 20000000000 | bytes 10000000 | tf_op jit(solution)/shard_map/join_parts/pallas_call | solution.py:145
  272.9 13.3 %all-to-all-done.4.refs_0_ = bf16[8,3,112,512]{3,2,1,0:T(8,128)(2,1)} async-done(((bf16[8,3,112,512]{3,2,1,0:T(8,128)(2,1)}), bf16[8,3,112,512]{3,2,1,0:T(8,128)(2,1)}, u32[]{:S(2)}, u32[]{:S(2)}) %all-to-all-start.4) | async-done | bytes 2752544 | tf_op jit(solution)/shard_map/all_to_all | solution.py:51
  286.2 4.0 %store.3 = (bf16[448,2048]{1,0:T(8,128)(2,1)}, bf16[448,2048]{1,0:T(8,128)(2,1)}, bf16[448,2048]{1,0:T(8,128)(2,1)}) custom-call(bf16[8,3,112,512]{3,2,1,0:T(8,128)(2,1)} %all-to-all-done.4.refs_0_, bf16[448,2048]{1,0:T(8,128)(2,1)} %get-tuple-element.162.refs_1_, ...), custom_call_target="tpu_custom_call", output_to_operand_aliasing={{0}: (1, {}), {1}: (2, {}), {2}: (3, {})} | custom-call | bytes 65536 | tf_op jit(solution)/shard_map/store/pallas_call | solution.py:357
  (115 shorter events, 53.1 us)
Async XLA Ops:
  7.2 78.2 %all-gather.8.cloned.1.call-start = ((), (), s32[]{:S(2)}) async-start(), calls=%async_computation.6 | async-start | bytes 3932160 | tf_op jit(solution)/shard_map/all_gather | solution.py:512
  22.9 40.5 %all-to-all-start = ((bf16[8,3,112,512]{3,2,1,0:T(8,128)(2,1)}), bf16[8,3,112,512]{3,2,1,0:T(8,128)(2,1)S(1)}, u32[]{:S(2)}, u32[]{:S(2)}) async-start(bf16[8,3,112,512]{3,2,1,0:T(8,128)(2,1)} %get-tuple-element.127), calls=%async_computation | async-start | bytes 5505024 | tf_op jit(solution)/shard_map/all_to_all | solution.py:51
  30.0 101.2 %all-gather.10.cloned.1.call-start = ((), (), s32[]{:S(2)}) async-start(), calls=%async_computation.7 | async-start | bytes 3932160 | tf_op jit(solution)/shard_map/all_gather | solution.py:512
  30.7 51.5 %collective-permute-start.7 = (bf16[448,2048]{1,0:T(8,128)(2,1)}, bf16[448,2048]{1,0:T(8,128)(2,1)}, u32[]{:S(2)}, u32[]{:S(2)}) collective-permute-start(bf16[448,2048]{1,0:T(8,128)(2,1)} %bitcast.54), channel_id=1, source_target_pairs={{0,4},{1,5},{2,6},{3,7},{4,0},{5,1},{6,2},{7,3},{8,12},{9,13},{10,... | collective-permute-start | bytes 5505032 | tf_op jit(solution)/shard_map/ppermute | solution.py:40
  33.5 33.8 %collective-permute-start.6 = (bf16[384,896]{1,0:T(8,128)(2,1)}, bf16[384,896]{1,0:T(8,128)(2,1)}, u32[]{:S(2)}, u32[]{:S(2)}) collective-permute-start(bf16[384,896]{1,0:T(8,128)(2,1)} %get-tuple-element.181), channel_id=1, source_target_pairs={{0,3},{1,0},{2,1},{3,2},{4,7},{5,4},{6,5},{7,6},{8,11},{9,8},{10,9... | collective-permute-start | bytes 2064392 | tf_op jit(solution)/shard_map/ppermute | solution.py:40
  36.3 31.4 %collective-permute-start.5 = (bf16[384,896]{1,0:T(8,128)(2,1)}, bf16[384,896]{1,0:T(8,128)(2,1)}, u32[]{:S(2)}, u32[]{:S(2)}) collective-permute-start(bf16[384,896]{1,0:T(8,128)(2,1)} %get-tuple-element.182), channel_id=1, source_target_pairs={{0,2},{1,3},{2,0},{3,1},{4,6},{5,7},{6,4},{7,5},{8,10},{9,11},{10,... | collective-permute-start | bytes 2064392 | tf_op jit(solution)/shard_map/ppermute | solution.py:40
  36.6 45.6 %collective-permute-start.4 = (bf16[384,896]{1,0:T(8,128)(2,1)S(1)}, bf16[384,896]{1,0:T(8,128)(2,1)}, u32[]{:S(2)}, u32[]{:S(2)}) collective-permute-start(bf16[384,896]{1,0:T(8,128)(2,1)S(1)} %get-tuple-element.183), channel_id=1, source_target_pairs={{0,1},{1,2},{2,3},{3,0},{4,5},{5,6},{6,7},{7,4},{8,9},{9,10},{10,1... | collective-permute-start | bytes 2064392 | tf_op jit(solution)/shard_map/ppermute | solution.py:40
  65.4 31.1 %collective-permute-start.8 = (bf16[3,3,112,512]{3,2,1,0:T(8,128)(2,1)}, bf16[3,3,112,512]{3,2,1,0:T(8,128)(2,1)}, u32[]{:S(2)}, u32[]{:S(2)}) collective-permute-start(bf16[3,3,112,512]{3,2,1,0:T(8,128)(2,1)} %take_pieces.12), channel_id=1, source_target_pairs={{0,16},{8,24},{16,0},{24,8},{32,48},{40,56},{48,32},{56,40},{64,80... | collective-permute-start | bytes 3096584 | tf_op jit(solution)/shard_map/ppermute | solution.py:47
  96.4 43.8 %all-to-all-start.1 = ((bf16[8,3,112,512]{3,2,1,0:T(8,128)(2,1)}), bf16[8,3,112,512]{3,2,1,0:T(8,128)(2,1)S(1)}, u32[]{:S(2)}, u32[]{:S(2)}) async-start(bf16[8,3,112,512]{3,2,1,0:T(8,128)(2,1)} %get-tuple-element.132), calls=%async_computation.1 | async-start | bytes 5505024 | tf_op jit(solution)/shard_map/all_to_all | solution.py:51
  102.9 23.6 %collective-permute-start.9 = (bf16[448,1024]{1,0:T(8,128)(2,1)S(1)}, bf16[448,1024]{1,0:T(8,128)(2,1)S(1)}, u32[]{:S(2)}, u32[]{:S(2)}) collective-permute-start(bf16[448,1024]{1,0:T(8,128)(2,1)S(1)} %slice.49), channel_id=1, source_target_pairs={{0,4},{1,5},{2,6},{3,7},{4,0},{5,1},{6,2},{7,3},{8,12},{9,13},{10,... | collective-permute-start | bytes 2752520 | tf_op jit(solution)/shard_map/ppermute | solution.py:40
  117.9 43.9 %collective-permute-start.11 = (bf16[384,2048]{1,0:T(8,128)(2,1)}, bf16[384,2048]{1,0:T(8,128)(2,1)}, u32[]{:S(2)}, u32[]{:S(2)}) collective-permute-start(bf16[384,2048]{1,0:T(8,128)(2,1)} %get-tuple-element.142), channel_id=1, source_target_pairs={{0,1},{1,2},{2,3},{3,0},{4,5},{5,6},{6,7},{7,4},{8,9},{9,10},{10,1... | collective-permute-start | bytes 4718600 | tf_op jit(solution)/shard_map/ppermute | solution.py:40
  119.2 42.5 %collective-permute-start.12 = (bf16[384,2048]{1,0:T(8,128)(2,1)}, bf16[384,2048]{1,0:T(8,128)(2,1)}, u32[]{:S(2)}, u32[]{:S(2)}) collective-permute-start(bf16[384,2048]{1,0:T(8,128)(2,1)} %get-tuple-element.143), channel_id=1, source_target_pairs={{0,3},{1,0},{2,1},{3,2},{4,7},{5,4},{6,5},{7,6},{8,11},{9,8},{10,9... | collective-permute-start | bytes 4718600 | tf_op jit(solution)/shard_map/ppermute | solution.py:40
  138.5 23.3 %collective-permute-start.10 = (bf16[448,1024]{1,0:T(8,128)(2,1)}, bf16[448,1024]{1,0:T(8,128)(2,1)}, u32[]{:S(2)}, u32[]{:S(2)}) collective-permute-start(bf16[448,1024]{1,0:T(8,128)(2,1)} %slice.50), channel_id=1, source_target_pairs={{0,4},{1,5},{2,6},{3,7},{4,0},{5,1},{6,2},{7,3},{8,12},{9,13},{10,... | collective-permute-start | bytes 2752520 | tf_op jit(solution)/shard_map/ppermute | solution.py:40
  140.2 50.5 %copy-start = (bf16[8,3,112,512]{3,2,1,0:T(8,128)(2,1)}, bf16[8,3,112,512]{3,2,1,0:T(8,128)(2,1)S(1)}, u32[]{:S(2)}) copy-start(bf16[8,3,112,512]{3,2,1,0:T(8,128)(2,1)S(1)} %all-to-all-done.1.pool_ref) | copy-start | bytes 8257540
  140.2 19.2 %all-to-all-start.2 = ((bf16[8,112,512]{2,1,0:T(8,128)(2,1)}), bf16[8,112,512]{2,1,0:T(8,128)(2,1)}, u32[]{:S(2)}, u32[]{:S(2)}) async-start(bf16[8,112,512]{2,1,0:T(8,128)(2,1)} %add_halves.2), calls=%async_computation.2 | async-start | bytes 1835008 | tf_op jit(solution)/shard_map/all_to_all | solution.py:51
  165.5 28.5 %all-to-all-start.3 = ((bf16[8,112,512]{2,1,0:T(8,128)(2,1)}), bf16[8,112,512]{2,1,0:T(8,128)(2,1)}, u32[]{:S(2)}, u32[]{:S(2)}) async-start(bf16[8,112,512]{2,1,0:T(8,128)(2,1)} %add_halves.3), calls=%async_computation.3 | async-start | bytes 1835008 | tf_op jit(solution)/shard_map/all_to_all | solution.py:51
  170.8 23.1 %collective-permute-start.20 = (bf16[384,1024]{1,0:T(8,128)(2,1)}, bf16[384,1024]{1,0:T(8,128)(2,1)}, u32[]{:S(2)}, u32[]{:S(2)}) collective-permute-start(bf16[384,1024]{1,0:T(8,128)(2,1)} %get-tuple-element.158), channel_id=1, source_target_pairs={{0,2},{1,3},{2,0},{3,1},{4,6},{5,7},{6,4},{7,5},{8,10},{9,11},{10,... | collective-permute-start | bytes 2359304 | tf_op jit(solution)/shard_map/ppermute | solution.py:40
  173.8 9.3 %collective-permute-start.13 = (bf16[3,112,512]{2,1,0:T(8,128)(2,1)S(1)}, bf16[3,112,512]{2,1,0:T(8,128)(2,1)S(1)}, u32[]{:S(2)}, u32[]{:S(2)}) collective-permute-start(bf16[3,112,512]{2,1,0:T(8,128)(2,1)S(1)} %copy-done.6), channel_id=1, source_target_pairs={{0,16},{8,24},{16,0},{24,8},{32,48},{40,56},{48,32},{56,40},{64,80... | collective-permute-start | bytes 1032200 | tf_op jit(solution)/shard_map/ppermute | solution.py:47
  192.7 25.2 %copy-start.7 = (f32[1,3584]{1,0:T(1,128)S(1)}, f32[1,3584]{1,0:T(1,128)}, u32[]{:S(2)}) copy-start(f32[1,3584]{1,0:T(1,128)} %gain_ref.2) | copy-start | bytes 43012
  192.7 25.1 %collective-permute-start.14 = (bf16[3,3,112,512]{3,2,1,0:T(8,128)(2,1)}, bf16[3,3,112,512]{3,2,1,0:T(8,128)(2,1)}, u32[]{:S(2)}, u32[]{:S(2)}) collective-permute-start(bf16[3,3,112,512]{3,2,1,0:T(8,128)(2,1)} %take_pieces.14), channel_id=1, source_target_pairs={{0,16},{8,24},{16,0},{24,8},{32,48},{40,56},{48,32},{56,40},{64,80... | collective-permute-start | bytes 3096584 | tf_op jit(solution)/shard_map/ppermute | solution.py:47
  194.0 45.3 %all-to-all-start.5 = ((bf16[8,3,112,512]{3,2,1,0:T(8,128)(2,1)}), bf16[8,3,112,512]{3,2,1,0:T(8,128)(2,1)S(1)}, u32[]{:S(2)}, u32[]{:S(2)}) async-start(bf16[8,3,112,512]{3,2,1,0:T(8,128)(2,1)} %get-tuple-element.193), calls=%async_computation.5 | async-start | bytes 5505024 | tf_op jit(solution)/shard_map/all_to_all | solution.py:51
  199.9 69.3 %all-gather.12.cloned.1.call-start = ((), (), s32[]{:S(2)}) async-start(), calls=%async_computation.8 | async-start | bytes 1949696 | tf_op jit(solution)/shard_map/all_gather | solution.py:578
  202.3 2.9 collective-permute-start.23
  203.1 4.3 %collective-permute-start.22 = (f32[2,448]{1,0:T(2,128)S(1)}, f32[2,448]{1,0:T(2,128)S(1)}, u32[]{:S(2)}, u32[]{:S(2)}) collective-permute-start(f32[2,448]{1,0:T(2,128)S(1)} %reshape.182), channel_id=1, source_target_pairs={{0,2},{1,3},{2,0},{3,1},{4,6},{5,7},{6,4},{7,5},{8,10},{9,11},{10,... | collective-permute-start | bytes 10760 | tf_op jit(solution)/shard_map/ppermute | solution.py:40
  204.7 4.0 %collective-permute-start.21 = (f32[2,448]{1,0:T(2,128)S(1)}, f32[2,448]{1,0:T(2,128)S(1)}, u32[]{:S(2)}, u32[]{:S(2)}) collective-permute-start(f32[2,448]{1,0:T(2,128)S(1)} %reshape.182), channel_id=1, source_target_pairs={{0,1},{1,2},{2,3},{3,0},{4,5},{5,6},{6,7},{7,4},{8,9},{9,10},{10,1... | collective-permute-start | bytes 10760 | tf_op jit(solution)/shard_map/ppermute | solution.py:40
  208.8 8.9 %collective-permute-start.24 = (f32[4,2,448]{2,0,1:T(4,128)S(1)}, f32[4,2,448]{2,0,1:T(4,128)S(1)}, u32[]{:S(2)}, u32[]{:S(2)}) collective-permute-start(f32[4,2,448]{2,0,1:T(4,128)S(1)} %dynamic_update_slice.16), channel_id=1, source_target_pairs={{0,4},{1,5},{2,6},{3,7},{4,0},{5,1},{6,2},{7,3},{8,12},{9,13},{10,... | collective-permute-start | bytes 43016 | tf_op jit(solution)/shard_map/ppermute | solution.py:40
  210.3 21.4 %collective-permute-start.16 = (bf16[384,1024]{1,0:T(8,128)(2,1)}, bf16[384,1024]{1,0:T(8,128)(2,1)}, u32[]{:S(2)}, u32[]{:S(2)}) collective-permute-start(bf16[384,1024]{1,0:T(8,128)(2,1)} %get-tuple-element.149), channel_id=1, source_target_pairs={{0,2},{1,3},{2,0},{3,1},{4,6},{5,7},{6,4},{7,5},{8,10},{9,11},{10,... | collective-permute-start | bytes 2359304 | tf_op jit(solution)/shard_map/ppermute | solution.py:40
  217.8 7.9 %collective-permute-start.15 = (bf16[3,112,512]{2,1,0:T(8,128)(2,1)}, bf16[3,112,512]{2,1,0:T(8,128)(2,1)S(1)}, u32[]{:S(2)}, u32[]{:S(2)}) collective-permute-start(bf16[3,112,512]{2,1,0:T(8,128)(2,1)} %take_pieces.15), channel_id=1, source_target_pairs={{0,16},{8,24},{16,0},{24,8},{32,48},{40,56},{48,32},{56,40},{64,80... | collective-permute-start | bytes 1032200 | tf_op jit(solution)/shard_map/ppermute | solution.py:47
  225.7 21.9 %collective-permute-start.17 = (bf16[384,896]{1,0:T(8,128)(2,1)}, bf16[384,896]{1,0:T(8,128)(2,1)}, u32[]{:S(2)}, u32[]{:S(2)}) collective-permute-start(bf16[384,896]{1,0:T(8,128)(2,1)} %get-tuple-element.153), channel_id=1, source_target_pairs={{0,1},{1,2},{2,3},{3,0},{4,5},{5,6},{6,7},{7,4},{8,9},{9,10},{10,1... | collective-permute-start | bytes 2064392 | tf_op jit(solution)/shard_map/ppermute | solution.py:40
  225.7 33.2 %collective-permute-start.18 = (bf16[384,896]{1,0:T(8,128)(2,1)}, bf16[384,896]{1,0:T(8,128)(2,1)}, u32[]{:S(2)}, u32[]{:S(2)}) collective-permute-start(bf16[384,896]{1,0:T(8,128)(2,1)} %get-tuple-element.155), channel_id=1, source_target_pairs={{0,2},{1,3},{2,0},{3,1},{4,6},{5,7},{6,4},{7,5},{8,10},{9,11},{10,... | collective-permute-start | bytes 2064392 | tf_op jit(solution)/shard_map/ppermute | solution.py:40
  227.7 31.2 %collective-permute-start.19 = (bf16[384,896]{1,0:T(8,128)(2,1)}, bf16[384,896]{1,0:T(8,128)(2,1)}, u32[]{:S(2)}, u32[]{:S(2)}) collective-permute-start(bf16[384,896]{1,0:T(8,128)(2,1)} %get-tuple-element.157), channel_id=1, source_target_pairs={{0,3},{1,0},{2,1},{3,2},{4,7},{5,4},{6,5},{7,6},{8,11},{9,8},{10,9... | collective-permute-start | bytes 2064392 | tf_op jit(solution)/shard_map/ppermute | solution.py:40
  239.3 46.9 %all-to-all-start.4 = ((bf16[8,3,112,512]{3,2,1,0:T(8,128)(2,1)}), bf16[8,3,112,512]{3,2,1,0:T(8,128)(2,1)}, u32[]{:S(2)}, u32[]{:S(2)}) async-start(bf16[8,3,112,512]{3,2,1,0:T(8,128)(2,1)} %get-tuple-element.194), calls=%async_computation.4 | async-start | bytes 5505024 | tf_op jit(solution)/shard_map/all_to_all | solution.py:51
  (9 other events, 125.4 us)
Sparse Core Ops, SparseCore 0:
  10.2 69.3 all-gather.7
  81.3 41.0 all-gather.9
  229.2 39.9 all-gather.11

commit v3 on v2

--- a/solution.py
+++ b/solution.py
@@ -31,7 +31,8 @@
     second_new = beta_two * second + (1.0 - beta_two) * grad * grad
     corr_one = 1.0 - beta_one**STEP
     corr_two = 1.0 - beta_two**STEP
-    step_dir = first_new / corr_one / (jnp.sqrt(second_new / corr_two) + adam_eps) + decay * param
+    scaled = jnp.sqrt(second_new * (1.0 / corr_two)) + adam_eps
+    step_dir = first_new * (1.0 / corr_one) / scaled + decay * param
     return (param - learn_rate * step_dir, first_new, second_new)
 
 
@@ -471,6 +472,13 @@
     )(y[None], x, *w)
 
 
+def last_used(index, used):
+    order = jnp.arange(index.shape[0], dtype=jnp.int32)
+    seen = used[None, :] & (order[None, :] <= order[:, None])
+    at = jnp.maximum(jnp.max(jnp.where(seen, order[None, :], -1), axis=1), 0)
+    return jnp.sum(jnp.where(at[:, None] == order[None, :], index[None, :], 0), axis=1)
+
+
 def shards(
     hidden,
     value_grad,
@@ -500,8 +508,10 @@
     place = lambda s: s // 4 * 2 + s % 2
     my_src, my_cross, my_slot = pick(src, xl), pick(cross, xl), pick(slot, xl)
     leaving = place(pick(slot_src, 1 - xl))
-    table = jnp.stack([my_cross, place(my_src), my_slot])
-    table_few = jnp.stack([my_cross, place(my_src), jnp.minimum(my_slot, SLOTS - 1)])
+    near_place = last_used(place(my_src), my_cross == 0)
+    far_slot = last_used(my_slot, my_cross == 1)
+    table = jnp.stack([my_cross, near_place, far_slot])
+    table_few = jnp.stack([my_cross, near_place, jnp.minimum(far_slot, SLOTS - 1)])
 
     blocks = split_inputs(hidden[0], norm_gain, xh)
     pieces = [pick(blocks, y_at[d]) for d in (1, 2, 3)]

time: 299 us -> 308 us (1.030)
  starting transfers between devices: 63.5 us -> 74.2 us
    all_to_all x6, starting transfers between devices: 36.8 us -> 43.4 us  [swap_members(): return lax.all_to_all(x, 'member', 0, 0, axis_index_groups=X_GROUPS)]
    ppermute x17, starting transfers between devices: 22.8 us -> 29 us  [to_fsdp(): return lax.ppermute(x, 'fsdp', pairs)]
  transfers between devices with their start and end apart: 30 -> 30, of which waited for: 15 -> 12; matrix products, arithmetic and copies ran while one was open for 8% -> 8% of each run, Pallas kernels for 27% -> 27%
where the time goes in v3:
time: 308 us; the launch traced here: 307 us
  waiting for transfers between devices  101 us (33%)
  Pallas kernels  86.4 us (28%)
  starting transfers between devices  74.2 us (24%)
  between operations  16.8 us (5%)
  matrix products  12.8 us (4%)
  local copies, waits for them, and re-layouts  11.7 us (4%)
  other arithmetic  4.02 us (1%)
    all_to_all x6, starting transfers between devices, swap_members(): return lax.all_to_all(x, 'member', 0, 0, axis_index_groups=X_GROUPS)  43.4 us
    ppermute x17, waiting for transfers between devices, to_fsdp(): return lax.ppermute(x, 'fsdp', pairs)  40.9 us
    all_to_all x6, waiting for transfers between devices, swap_members(): return lax.all_to_all(x, 'member', 0, 0, axis_index_groups=X_GROUPS)  38.6 us
    ppermute x17, starting transfers between devices, to_fsdp(): return lax.ppermute(x, 'fsdp', pairs)  29 us
    ppermute x4, waiting for transfers between devices, to_member(): return lax.ppermute(x, 'member', pairs)  20.6 us
    pallas_call x2, Pallas kernels, adam_of_sources(): pl.pallas_call(adam_kernel, grid_spec=pltpu.PrefetchScalarGridSpec(num_sc...  15.1 us
    pallas_call x1, Pallas kernels, input_grads(): pl.pallas_call(input_grad_kernel, grid_spec=pltpu.PrefetchScalarGridSpec(...  13.3 us
    pallas_call x1, Pallas kernels, value_parts(): pl.pallas_call(value_kernel, grid_spec=pltpu.PrefetchScalarGridSpec(num_s...  13.2 us
  transfers between devices with their start and end apart: 30, of which 12 were waited for; matrix products, arithmetic and copies ran while one was open for 8% of the time, Pallas kernels for 27%

profile of v3, /device:TPU:1, one launch (start us, length us, event | category | flops | bytes accessed | tf_op | source)
XLA Modules:
  0.0 306.8 jit_solution(8031045362738410269)
XLA Ops:
  9.9 4.8 %split_inputs.1.refs_3_ = bf16[4,384,896]{2,1,0:T(8,128)(2,1)} custom-call(s32[1]{0:T(128)} %bitcast.xh_ref, bf16[384,3584]{1,0:T(8,128)(2,1)} %bitcast.71, f32[1,3584]{1,0:T(1,128)} %gain_ref.2), custom_call_target="tpu_custom_call" | custom-call | bytes 65536 | tf_op jit(solution)/shard_map/split_inputs/pallas_call | solution.py:93
  17.5 5.4 %spread_states.1 = (bf16[8,3,112,512]{3,2,1,0:T(8,128)(2,1)}, bf16[8,3,112,512]{3,2,1,0:T(8,128)(2,1)}) custom-call(bf16[448,2048]{1,0:T(8,128)(2,1)} %bitcast.64, bf16[448,2048]{1,0:T(8,128)(2,1)} %bitcast.73, bf16[448,2048]{1,0:T(8,128)(2,1)} %bitcast.74), custom_call_target="tpu_custom_call" | custom-call | bytes 65536 | tf_op jit(solution)/shard_map/spread_states/pallas_call | solution.py:185
  22.9 7.1 %all-to-all-start = ((bf16[8,3,112,512]{3,2,1,0:T(8,128)(2,1)}), bf16[8,3,112,512]{3,2,1,0:T(8,128)(2,1)S(1)}, u32[]{:S(2)}, u32[]{:S(2)}) async-start(bf16[8,3,112,512]{3,2,1,0:T(8,128)(2,1)} %get-tuple-element.127), calls=%async_computation | async-start | bytes 5505024 | tf_op jit(solution)/shard_map/all_to_all | solution.py:52
  38.1 25.3 %all-to-all-done.pool_ref = bf16[8,3,112,512]{3,2,1,0:T(8,128)(2,1)S(1)} async-done(((bf16[8,3,112,512]{3,2,1,0:T(8,128)(2,1)}), bf16[8,3,112,512]{3,2,1,0:T(8,128)(2,1)S(1)}, u32[]{:S(2)}, u32[]{:S(2)}) %all-to-all-start) | async-done | bytes 2752544 | tf_op jit(solution)/shard_map/all_to_all | solution.py:52
  67.7 14.5 %collective-permute-done.4.refs_0_ = bf16[384,896]{1,0:T(8,128)(2,1)} collective-permute-done((bf16[384,896]{1,0:T(8,128)(2,1)S(1)}, bf16[384,896]{1,0:T(8,128)(2,1)}, u32[]{:S(2)}, u32[]{:S(2)}) %collective-permute-start.4) | collective-permute-done | bytes 688160 | tf_op jit(solution)/shard_map/ppermute | solution.py:41
  85.4 7.0 %convolution_convert_fusion.1.here_ref = bf16[896,1024]{1,0:T(8,128)(2,1)} fusion(bf16[1536,896]{1,0:T(8,128)(2,1)} %bitcast.60, bf16[1,1536,1024]{2,1,0:T(8,128)(2,1)} %all-gather.8.cloned.1.call-done), kind=kOutput, calls=%fused_computation.5 | convolution fusion | flops 2819489792 | bytes 7733248 | tf_op jit(solution)/shard_map/dot_general | solution.py:68
  92.4 4.1 %collective-permute-done.8 = bf16[3,3,112,512]{3,2,1,0:T(8,128)(2,1)} collective-permute-done((bf16[3,3,112,512]{3,2,1,0:T(8,128)(2,1)}, bf16[3,3,112,512]{3,2,1,0:T(8,128)(2,1)}, u32[]{:S(2)}, u32[]{:S(2)}) %collective-permute-start.8) | collective-permute-done | bytes 1032224 | tf_op jit(solution)/shard_map/ppermute | solution.py:48
  96.5 5.2 %all-to-all-start.1 = ((bf16[8,3,112,512]{3,2,1,0:T(8,128)(2,1)}), bf16[8,3,112,512]{3,2,1,0:T(8,128)(2,1)S(1)}, u32[]{:S(2)}, u32[]{:S(2)}) async-start(bf16[8,3,112,512]{3,2,1,0:T(8,128)(2,1)} %get-tuple-element.132), calls=%async_computation.1 | async-start | bytes 5505024 | tf_op jit(solution)/shard_map/all_to_all | solution.py:52
  105.6 13.2 %value_parts.1 = (bf16[384,2048]{1,0:T(8,128)(2,1)}, bf16[384,2048]{1,0:T(8,128)(2,1)}, bf16[384,1024]{1,0:T(8,128)(2,1)}, bf16[384,1024]{1,0:T(8,128)(2,1)}, bf16[384,2048]{1,0:T(8,128)(2,1)}) custom-call(s32[1]{0:T(128)} %bitcast.1.y_ref, bf16[1536,896]{1,0:T(8,128)(2,1)} %bitcast.61, bf16[448,2048]{1,0:T(8,128)(2,1)} %bitcast.66, ...), custom_call_target="tpu_custom_call" | custom-call | bytes 65536 | tf_op jit(solution)/shard_map/value_parts/pallas_call | solution.py:458
  121.5 6.2 %collective-permute-done.9.came_ref = bf16[448,1024]{1,0:T(8,128)(2,1)} collective-permute-done((bf16[448,1024]{1,0:T(8,128)(2,1)}, bf16[448,1024]{1,0:T(8,128)(2,1)}, u32[]{:S(2)}, u32[]{:S(2)}) %collective-permute-start.9) | collective-permute-done | bytes 917536 | tf_op jit(solution)/shard_map/ppermute | solution.py:41
  127.7 3.6 %add_halves.2 = bf16[8,112,512]{2,1,0:T(8,128)(2,1)} custom-call(bf16[896,1024]{1,0:T(8,128)(2,1)} %convolution_convert_fusion.1.here_ref, bf16[448,1024]{1,0:T(8,128)(2,1)} %collective-permute-done.9.came_ref), custom_call_target="tpu_custom_call" | custom-call | bytes 65536 | tf_op jit(solution)/shard_map/add_halves/pallas_call | solution.py:207
  131.3 5.8 %convolution_convert_fusion.here_ref = bf16[896,1024]{1,0:T(8,128)(2,1)S(1)} fusion(bf16[1536,896]{1,0:T(8,128)(2,1)} %bitcast.62, bf16[1536,1024]{1,0:T(8,128)(2,1)} %bitcast.69), kind=kOutput, calls=%fused_computation.4 | convolution fusion | flops 2819489792 | bytes 7733248 | tf_op jit(solution)/shard_map/dot_general | solution.py:68
  139.9 5.5 %all-to-all-start.2 = ((bf16[8,112,512]{2,1,0:T(8,128)(2,1)}), bf16[8,112,512]{2,1,0:T(8,128)(2,1)}, u32[]{:S(2)}, u32[]{:S(2)}) async-start(bf16[8,112,512]{2,1,0:T(8,128)(2,1)} %add_halves.2), calls=%async_computation.2 | async-start | bytes 1835008 | tf_op jit(solution)/shard_map/all_to_all | solution.py:52
  149.0 13.3 %input_grads.1 = (bf16[384,896]{1,0:T(8,128)(2,1)}, bf16[384,896]{1,0:T(8,128)(2,1)}, bf16[384,896]{1,0:T(8,128)(2,1)}, bf16[384,896]{1,0:T(8,128)(2,1)}, f32[1,896]{1,0:T(1,128)}) custom-call(s32[1]{0:T(128)} %bitcast.1.y_ref, bf16[1536,1024]{1,0:T(8,128)(2,1)} %bitcast.68, bf16[1536,1024]{1,0:T(8,128)(2,1)} %bitcast.70, bf16[448,2048]{1,0:T(8,128)(2,1)} %bitcast.67, ...), custom_call_target="tpu_custom_call" | custom-call | bytes 65536 | tf_op jit(solution)/shard_map/input_grads/pallas_call | solution.py:414
  164.6 3.7 %add_halves.3 = bf16[8,112,512]{2,1,0:T(8,128)(2,1)} custom-call(bf16[896,1024]{1,0:T(8,128)(2,1)} %copy-done.4, bf16[448,1024]{1,0:T(8,128)(2,1)} %collective-permute-done.10.came_ref), custom_call_target="tpu_custom_call" | custom-call | bytes 65536 | tf_op jit(solution)/shard_map/add_halves/pallas_call | solution.py:207
  168.3 13.2 %all-to-all-start.3 = ((bf16[8,112,512]{2,1,0:T(8,128)(2,1)}), bf16[8,112,512]{2,1,0:T(8,128)(2,1)}, u32[]{:S(2)}, u32[]{:S(2)}) async-start(bf16[8,112,512]{2,1,0:T(8,128)(2,1)} %add_halves.3), calls=%async_computation.3 | async-start | bytes 1835008 | tf_op jit(solution)/shard_map/all_to_all | solution.py:52
  183.2 8.3 %collective-permute-done.13 = bf16[3,112,512]{2,1,0:T(8,128)(2,1)S(1)} collective-permute-done((bf16[3,112,512]{2,1,0:T(8,128)(2,1)S(1)}, bf16[3,112,512]{2,1,0:T(8,128)(2,1)S(1)}, u32[]{:S(2)}, u32[]{:S(2)}) %collective-permute-start.13) | collective-permute-done | bytes 344096 | tf_op jit(solution)/shard_map/ppermute | solution.py:48
  191.5 7.5 %conditional.2 = (bf16[8,3,112,512]{3,2,1,0:T(8,128)(2,1)}) conditional(s32[]{:T(128)} %convert_element_type.35, (s32[3,8]{1,0:T(4,128)S(1)}, bf16[8,3,112,512]{3,2,1,0:T(8,128)(2,1)}, bf16[8,112,512]{2,1,0:T(8,128)(2,1)}, bf16[3,3,112,512]{3,2,1,0:T(8,128)(2,1)}, bf16[3,112,512]{2,1,0:T(8,128)(2,1)S(1)}) %tuple.91, (s32[8]{0:T(128)S(1)}, ...), branch_computations={%region_10.11_spmd, %region_11.12_spmd} | conditional | flops 1835008 | bytes 27721884 | solution.py:552
  191.5 7.5 %adam_of_sources.4 = bf16[8,3,112,512]{3,2,1,0:T(8,128)(2,1)} custom-call(s32[3,8]{1,0:T(4,128)S(1)} %get-tuple-element.26.table_ref, bf16[8,3,112,512]{3,2,1,0:T(8,128)(2,1)} %get-tuple-element.44.refs_0_, bf16[8,112,512]{2,1,0:T(8,128)(2,1)} %get-tuple-element.52.refs_1_, bf16[3,3,112,512]{3,2,1,0:T(8,128)(2,1)} %get-tuple-element.53.refs_2_, ...), custom_call_target="tpu_custom_call" | custom-call | bytes 65536 | tf_op jit(solution)/shard_map/cond/branch_0_fun/adam_of_sources/pallas_call | solution.py:316
  201.3 5.3 %all-to-all-start.5 = ((bf16[8,3,112,512]{3,2,1,0:T(8,128)(2,1)}), bf16[8,3,112,512]{3,2,1,0:T(8,128)(2,1)S(1)}, u32[]{:S(2)}, u32[]{:S(2)}) async-start(bf16[8,3,112,512]{3,2,1,0:T(8,128)(2,1)} %get-tuple-element.195), calls=%async_computation.5 | async-start | bytes 5505024 | tf_op jit(solution)/shard_map/all_to_all | solution.py:52
  209.0 3.4 %collective-permute-start.23 = (f32[2,448]{1,0:T(2,128)S(1)}, f32[2,448]{1,0:T(2,128)S(1)}, u32[]{:S(2)}, u32[]{:S(2)}) collective-permute-start(f32[2,448]{1,0:T(2,128)S(1)} %reshape.195), channel_id=1, source_target_pairs={{0,3},{1,0},{2,1},{3,2},{4,7},{5,4},{6,5},{7,6},{8,11},{9,8},{10,9... | collective-permute-start | bytes 10760 | tf_op jit(solution)/shard_map/ppermute | solution.py:41
  213.2 3.4 %collective-permute-done.22 = f32[2,448]{1,0:T(2,128)S(1)} collective-permute-done((f32[2,448]{1,0:T(2,128)S(1)}, f32[2,448]{1,0:T(2,128)S(1)}, u32[]{:S(2)}, u32[]{:S(2)}) %collective-permute-start.22) | collective-permute-done | bytes 3616 | tf_op jit(solution)/shard_map/ppermute | solution.py:41
  221.5 5.6 %collective-permute-done.24 = f32[4,2,448]{2,0,1:T(4,128)S(1)} collective-permute-done((f32[4,2,448]{2,0,1:T(4,128)S(1)}, f32[4,2,448]{2,0,1:T(4,128)S(1)}, u32[]{:S(2)}, u32[]{:S(2)}) %collective-permute-start.24) | collective-permute-done | bytes 14368 | tf_op jit(solution)/shard_map/ppermute | solution.py:41
  227.4 8.3 %collective-permute-done.15 = bf16[3,112,512]{2,1,0:T(8,128)(2,1)S(1)} collective-permute-done((bf16[3,112,512]{2,1,0:T(8,128)(2,1)}, bf16[3,112,512]{2,1,0:T(8,128)(2,1)S(1)}, u32[]{:S(2)}, u32[]{:S(2)}) %collective-permute-start.15) | collective-permute-done | bytes 344096 | tf_op jit(solution)/shard_map/ppermute | solution.py:48
  235.7 4.6 %collective-permute-start.18 = (bf16[384,896]{1,0:T(8,128)(2,1)}, bf16[384,896]{1,0:T(8,128)(2,1)}, u32[]{:S(2)}, u32[]{:S(2)}) collective-permute-start(bf16[384,896]{1,0:T(8,128)(2,1)} %get-tuple-element.155), channel_id=1, source_target_pairs={{0,2},{1,3},{2,0},{3,1},{4,6},{5,7},{6,4},{7,5},{8,10},{9,11},{10,... | collective-permute-start | bytes 2064392 | tf_op jit(solution)/shard_map/ppermute | solution.py:41
  243.5 7.6 %conditional.3 = (bf16[8,3,112,512]{3,2,1,0:T(8,128)(2,1)}) conditional(s32[]{:T(128)} %convert_element_type.35, (s32[3,8]{1,0:T(4,128)S(1)}, bf16[8,3,112,512]{3,2,1,0:T(8,128)(2,1)}, bf16[8,112,512]{2,1,0:T(8,128)(2,1)}, bf16[3,3,112,512]{3,2,1,0:T(8,128)(2,1)}, bf16[3,112,512]{2,1,0:T(8,128)(2,1)S(1)}) %tuple.89, (s32[8]{0:T(128)S(1)}, ...), branch_computations={%region_12.13_spmd, %region_13.14_spmd} | conditional | flops 1835008 | bytes 27721884 | solution.py:552
  243.5 7.6 %adam_of_sources.6 = bf16[8,3,112,512]{3,2,1,0:T(8,128)(2,1)} custom-call(s32[3,8]{1,0:T(4,128)S(1)} %get-tuple-element.61.table_ref, bf16[8,3,112,512]{3,2,1,0:T(8,128)(2,1)} %get-tuple-element.62.refs_0_, bf16[8,112,512]{2,1,0:T(8,128)(2,1)} %get-tuple-element.63.refs_1_, bf16[3,3,112,512]{3,2,1,0:T(8,128)(2,1)} %get-tuple-element.64.refs_2_, ...), custom_call_target="tpu_custom_call" | custom-call | bytes 65536 | tf_op jit(solution)/shard_map/cond/branch_0_fun/adam_of_sources/pallas_call | solution.py:316
  251.1 7.1 %all-to-all-start.4 = ((bf16[8,3,112,512]{3,2,1,0:T(8,128)(2,1)}), bf16[8,3,112,512]{3,2,1,0:T(8,128)(2,1)}, u32[]{:S(2)}, u32[]{:S(2)}) async-start(bf16[8,3,112,512]{3,2,1,0:T(8,128)(2,1)} %get-tuple-element.196), calls=%async_computation.4 | async-start | bytes 5505024 | tf_op jit(solution)/shard_map/all_to_all | solution.py:52
  258.8 9.7 %collective-permute-done.18.refs_2_ = bf16[384,896]{1,0:T(8,128)(2,1)} collective-permute-done((bf16[384,896]{1,0:T(8,128)(2,1)}, bf16[384,896]{1,0:T(8,128)(2,1)}, u32[]{:S(2)}, u32[]{:S(2)}) %collective-permute-start.18) | collective-permute-done | bytes 688160 | tf_op jit(solution)/shard_map/ppermute | solution.py:41
  269.6 9.7 %join_parts.1 = (bf16[384,3584]{1,0:T(8,128)(2,1)}, bf16[384,2048]{1,0:T(8,128)(2,1)}) custom-call(s32[2]{0:T(128)} %pad_add_fusion.3.place_ref, bf16[384,3584]{1,0:T(8,128)(2,1)} %bitcast.72, f32[1,3584]{1,0:T(1,128)} %gain_ref.2, bf16[384,896]{1,0:T(8,128)(2,1)} %get-tuple-element.140.refs_0_, bf16[384,896]{1,0:T(8,128)(2,1)} %collective-permute-done.17.refs_1_, ...), custom_call_target="tpu_custom_call" | custom-call | flops 20000000000 | bytes 10000000 | tf_op jit(solution)/shard_map/join_parts/pallas_call | solution.py:146
  283.0 13.3 %all-to-all-done.4.refs_0_ = bf16[8,3,112,512]{3,2,1,0:T(8,128)(2,1)} async-done(((bf16[8,3,112,512]{3,2,1,0:T(8,128)(2,1)}), bf16[8,3,112,512]{3,2,1,0:T(8,128)(2,1)}, u32[]{:S(2)}, u32[]{:S(2)}) %all-to-all-start.4) | async-done | bytes 2752544 | tf_op jit(solution)/shard_map/all_to_all | solution.py:52
  296.3 4.0 %store.3 = (bf16[448,2048]{1,0:T(8,128)(2,1)}, bf16[448,2048]{1,0:T(8,128)(2,1)}, bf16[448,2048]{1,0:T(8,128)(2,1)}) custom-call(bf16[8,3,112,512]{3,2,1,0:T(8,128)(2,1)} %all-to-all-done.4.refs_0_, bf16[448,2048]{1,0:T(8,128)(2,1)} %get-tuple-element.162.refs_1_, ...), custom_call_target="tpu_custom_call", output_to_operand_aliasing={{0}: (1, {}), {1}: (2, {}), {2}: (3, {})} | custom-call | bytes 65536 | tf_op jit(solution)/shard_map/store/pallas_call | solution.py:358
  (120 shorter events, 54.5 us)
Async XLA Ops:
  7.2 78.2 %all-gather.8.cloned.1.call-start = ((), (), s32[]{:S(2)}) async-start(), calls=%async_computation.6 | async-start | bytes 3932160 | tf_op jit(solution)/shard_map/all_gather | solution.py:522
  22.9 40.5 %all-to-all-start = ((bf16[8,3,112,512]{3,2,1,0:T(8,128)(2,1)}), bf16[8,3,112,512]{3,2,1,0:T(8,128)(2,1)S(1)}, u32[]{:S(2)}, u32[]{:S(2)}) async-start(bf16[8,3,112,512]{3,2,1,0:T(8,128)(2,1)} %get-tuple-element.127), calls=%async_computation | async-start | bytes 5505024 | tf_op jit(solution)/shard_map/all_to_all | solution.py:52
  30.0 101.4 %all-gather.10.cloned.1.call-start = ((), (), s32[]{:S(2)}) async-start(), calls=%async_computation.7 | async-start | bytes 3932160 | tf_op jit(solution)/shard_map/all_gather | solution.py:522
  30.7 51.5 %collective-permute-start.7 = (bf16[448,2048]{1,0:T(8,128)(2,1)}, bf16[448,2048]{1,0:T(8,128)(2,1)}, u32[]{:S(2)}, u32[]{:S(2)}) collective-permute-start(bf16[448,2048]{1,0:T(8,128)(2,1)} %bitcast.65), channel_id=1, source_target_pairs={{0,4},{1,5},{2,6},{3,7},{4,0},{5,1},{6,2},{7,3},{8,12},{9,13},{10,... | collective-permute-start | bytes 5505032 | tf_op jit(solution)/shard_map/ppermute | solution.py:41
  33.5 33.8 %collective-permute-start.6 = (bf16[384,896]{1,0:T(8,128)(2,1)}, bf16[384,896]{1,0:T(8,128)(2,1)}, u32[]{:S(2)}, u32[]{:S(2)}) collective-permute-start(bf16[384,896]{1,0:T(8,128)(2,1)} %get-tuple-element.181), channel_id=1, source_target_pairs={{0,3},{1,0},{2,1},{3,2},{4,7},{5,4},{6,5},{7,6},{8,11},{9,8},{10,9... | collective-permute-start | bytes 2064392 | tf_op jit(solution)/shard_map/ppermute | solution.py:41
  36.3 31.4 %collective-permute-start.5 = (bf16[384,896]{1,0:T(8,128)(2,1)}, bf16[384,896]{1,0:T(8,128)(2,1)}, u32[]{:S(2)}, u32[]{:S(2)}) collective-permute-start(bf16[384,896]{1,0:T(8,128)(2,1)} %get-tuple-element.182), channel_id=1, source_target_pairs={{0,2},{1,3},{2,0},{3,1},{4,6},{5,7},{6,4},{7,5},{8,10},{9,11},{10,... | collective-permute-start | bytes 2064392 | tf_op jit(solution)/shard_map/ppermute | solution.py:41
  36.6 45.6 %collective-permute-start.4 = (bf16[384,896]{1,0:T(8,128)(2,1)S(1)}, bf16[384,896]{1,0:T(8,128)(2,1)}, u32[]{:S(2)}, u32[]{:S(2)}) collective-permute-start(bf16[384,896]{1,0:T(8,128)(2,1)S(1)} %get-tuple-element.183), channel_id=1, source_target_pairs={{0,1},{1,2},{2,3},{3,0},{4,5},{5,6},{6,7},{7,4},{8,9},{9,10},{10,1... | collective-permute-start | bytes 2064392 | tf_op jit(solution)/shard_map/ppermute | solution.py:41
  65.5 31.0 %collective-permute-start.8 = (bf16[3,3,112,512]{3,2,1,0:T(8,128)(2,1)}, bf16[3,3,112,512]{3,2,1,0:T(8,128)(2,1)}, u32[]{:S(2)}, u32[]{:S(2)}) collective-permute-start(bf16[3,3,112,512]{3,2,1,0:T(8,128)(2,1)} %take_pieces.12), channel_id=1, source_target_pairs={{0,16},{8,24},{16,0},{24,8},{32,48},{40,56},{48,32},{56,40},{64,80... | collective-permute-start | bytes 3096584 | tf_op jit(solution)/shard_map/ppermute | solution.py:48
  96.5 43.4 %all-to-all-start.1 = ((bf16[8,3,112,512]{3,2,1,0:T(8,128)(2,1)}), bf16[8,3,112,512]{3,2,1,0:T(8,128)(2,1)S(1)}, u32[]{:S(2)}, u32[]{:S(2)}) async-start(bf16[8,3,112,512]{3,2,1,0:T(8,128)(2,1)} %get-tuple-element.132), calls=%async_computation.1 | async-start | bytes 5505024 | tf_op jit(solution)/shard_map/all_to_all | solution.py:52
  103.9 23.8 %collective-permute-start.9 = (bf16[448,1024]{1,0:T(8,128)(2,1)}, bf16[448,1024]{1,0:T(8,128)(2,1)}, u32[]{:S(2)}, u32[]{:S(2)}) collective-permute-start(bf16[448,1024]{1,0:T(8,128)(2,1)} %slice.49), channel_id=1, source_target_pairs={{0,4},{1,5},{2,6},{3,7},{4,0},{5,1},{6,2},{7,3},{8,12},{9,13},{10,... | collective-permute-start | bytes 2752520 | tf_op jit(solution)/shard_map/ppermute | solution.py:41
  118.8 45.8 %collective-permute-start.11 = (bf16[384,2048]{1,0:T(8,128)(2,1)}, bf16[384,2048]{1,0:T(8,128)(2,1)}, u32[]{:S(2)}, u32[]{:S(2)}) collective-permute-start(bf16[384,2048]{1,0:T(8,128)(2,1)} %get-tuple-element.142), channel_id=1, source_target_pairs={{0,1},{1,2},{2,3},{3,0},{4,5},{5,6},{6,7},{7,4},{8,9},{9,10},{10,1... | collective-permute-start | bytes 4718600 | tf_op jit(solution)/shard_map/ppermute | solution.py:41
  120.0 44.6 %collective-permute-start.12 = (bf16[384,2048]{1,0:T(8,128)(2,1)}, bf16[384,2048]{1,0:T(8,128)(2,1)}, u32[]{:S(2)}, u32[]{:S(2)}) collective-permute-start(bf16[384,2048]{1,0:T(8,128)(2,1)} %get-tuple-element.143), channel_id=1, source_target_pairs={{0,3},{1,0},{2,1},{3,2},{4,7},{5,4},{6,5},{7,6},{8,11},{9,8},{10,9... | collective-permute-start | bytes 4718600 | tf_op jit(solution)/shard_map/ppermute | solution.py:41
  138.2 26.4 %collective-permute-start.10 = (bf16[448,1024]{1,0:T(8,128)(2,1)}, bf16[448,1024]{1,0:T(8,128)(2,1)}, u32[]{:S(2)}, u32[]{:S(2)}) collective-permute-start(bf16[448,1024]{1,0:T(8,128)(2,1)} %slice.50), channel_id=1, source_target_pairs={{0,4},{1,5},{2,6},{3,7},{4,0},{5,1},{6,2},{7,3},{8,12},{9,13},{10,... | collective-permute-start | bytes 2752520 | tf_op jit(solution)/shard_map/ppermute | solution.py:41
  139.9 59.1 %copy-start = (bf16[8,3,112,512]{3,2,1,0:T(8,128)(2,1)}, bf16[8,3,112,512]{3,2,1,0:T(8,128)(2,1)S(1)}, u32[]{:S(2)}) copy-start(bf16[8,3,112,512]{3,2,1,0:T(8,128)(2,1)S(1)} %all-to-all-done.1.pool_ref) | copy-start | bytes 8257540
  139.9 22.4 %all-to-all-start.2 = ((bf16[8,112,512]{2,1,0:T(8,128)(2,1)}), bf16[8,112,512]{2,1,0:T(8,128)(2,1)}, u32[]{:S(2)}, u32[]{:S(2)}) async-start(bf16[8,112,512]{2,1,0:T(8,128)(2,1)} %add_halves.2), calls=%async_computation.2 | async-start | bytes 1835008 | tf_op jit(solution)/shard_map/all_to_all | solution.py:52
  146.0 55.3 %collective-permute-start.20 = (bf16[384,1024]{1,0:T(8,128)(2,1)}, bf16[384,1024]{1,0:T(8,128)(2,1)}, u32[]{:S(2)}, u32[]{:S(2)}) collective-permute-start(bf16[384,1024]{1,0:T(8,128)(2,1)} %get-tuple-element.158), channel_id=1, source_target_pairs={{0,2},{1,3},{2,0},{3,1},{4,6},{5,7},{6,4},{7,5},{8,10},{9,11},{10,... | collective-permute-start | bytes 2359304 | tf_op jit(solution)/shard_map/ppermute | solution.py:41
  168.3 33.0 %all-to-all-start.3 = ((bf16[8,112,512]{2,1,0:T(8,128)(2,1)}), bf16[8,112,512]{2,1,0:T(8,128)(2,1)}, u32[]{:S(2)}, u32[]{:S(2)}) async-start(bf16[8,112,512]{2,1,0:T(8,128)(2,1)} %add_halves.3), calls=%async_computation.3 | async-start | bytes 1835008 | tf_op jit(solution)/shard_map/all_to_all | solution.py:52
  181.6 9.9 %collective-permute-start.13 = (bf16[3,112,512]{2,1,0:T(8,128)(2,1)S(1)}, bf16[3,112,512]{2,1,0:T(8,128)(2,1)S(1)}, u32[]{:S(2)}, u32[]{:S(2)}) collective-permute-start(bf16[3,112,512]{2,1,0:T(8,128)(2,1)S(1)} %copy-done.5), channel_id=1, source_target_pairs={{0,16},{8,24},{16,0},{24,8},{32,48},{40,56},{48,32},{56,40},{64,80... | collective-permute-start | bytes 1032200 | tf_op jit(solution)/shard_map/ppermute | solution.py:48
  201.0 26.3 %copy-start.6 = (f32[1,3584]{1,0:T(1,128)S(1)}, f32[1,3584]{1,0:T(1,128)}, u32[]{:S(2)}) copy-start(f32[1,3584]{1,0:T(1,128)} %gain_ref.2) | copy-start | bytes 43012
  201.0 26.2 %collective-permute-start.14 = (bf16[3,3,112,512]{3,2,1,0:T(8,128)(2,1)}, bf16[3,3,112,512]{3,2,1,0:T(8,128)(2,1)}, u32[]{:S(2)}, u32[]{:S(2)}) collective-permute-start(bf16[3,3,112,512]{3,2,1,0:T(8,128)(2,1)} %take_pieces.14), channel_id=1, source_target_pairs={{0,16},{8,24},{16,0},{24,8},{32,48},{40,56},{48,32},{56,40},{64,80... | collective-permute-start | bytes 3096584 | tf_op jit(solution)/shard_map/ppermute | solution.py:48
  201.3 49.8 %all-to-all-start.5 = ((bf16[8,3,112,512]{3,2,1,0:T(8,128)(2,1)}), bf16[8,3,112,512]{3,2,1,0:T(8,128)(2,1)S(1)}, u32[]{:S(2)}, u32[]{:S(2)}) async-start(bf16[8,3,112,512]{3,2,1,0:T(8,128)(2,1)} %get-tuple-element.195), calls=%async_computation.5 | async-start | bytes 5505024 | tf_op jit(solution)/shard_map/all_to_all | solution.py:52
  206.6 72.7 %all-gather.12.cloned.1.call-start = ((), (), s32[]{:S(2)}) async-start(), calls=%async_computation.8 | async-start | bytes 1949696 | tf_op jit(solution)/shard_map/all_gather | solution.py:588
  209.0 4.2 %collective-permute-start.23 = (f32[2,448]{1,0:T(2,128)S(1)}, f32[2,448]{1,0:T(2,128)S(1)}, u32[]{:S(2)}, u32[]{:S(2)}) collective-permute-start(f32[2,448]{1,0:T(2,128)S(1)} %reshape.195), channel_id=1, source_target_pairs={{0,3},{1,0},{2,1},{3,2},{4,7},{5,4},{6,5},{7,6},{8,11},{9,8},{10,9... | collective-permute-start | bytes 10760 | tf_op jit(solution)/shard_map/ppermute | solution.py:41
  212.4 4.3 %collective-permute-start.22 = (f32[2,448]{1,0:T(2,128)S(1)}, f32[2,448]{1,0:T(2,128)S(1)}, u32[]{:S(2)}, u32[]{:S(2)}) collective-permute-start(f32[2,448]{1,0:T(2,128)S(1)} %reshape.195), channel_id=1, source_target_pairs={{0,2},{1,3},{2,0},{3,1},{4,6},{5,7},{6,4},{7,5},{8,10},{9,11},{10,... | collective-permute-start | bytes 10760 | tf_op jit(solution)/shard_map/ppermute | solution.py:41
  212.4 4.3 %collective-permute-start.21 = (f32[2,448]{1,0:T(2,128)S(1)}, f32[2,448]{1,0:T(2,128)S(1)}, u32[]{:S(2)}, u32[]{:S(2)}) collective-permute-start(f32[2,448]{1,0:T(2,128)S(1)} %reshape.195), channel_id=1, source_target_pairs={{0,1},{1,2},{2,3},{3,0},{4,5},{5,6},{6,7},{7,4},{8,9},{9,10},{10,1... | collective-permute-start | bytes 10760 | tf_op jit(solution)/shard_map/ppermute | solution.py:41
  216.8 10.2 %collective-permute-start.24 = (f32[4,2,448]{2,0,1:T(4,128)S(1)}, f32[4,2,448]{2,0,1:T(4,128)S(1)}, u32[]{:S(2)}, u32[]{:S(2)}) collective-permute-start(f32[4,2,448]{2,0,1:T(4,128)S(1)} %dynamic_update_slice.16), channel_id=1, source_target_pairs={{0,4},{1,5},{2,6},{3,7},{4,0},{5,1},{6,2},{7,3},{8,12},{9,13},{10,... | collective-permute-start | bytes 43016 | tf_op jit(solution)/shard_map/ppermute | solution.py:41
  219.9 23.6 %collective-permute-start.16 = (bf16[384,1024]{1,0:T(8,128)(2,1)}, bf16[384,1024]{1,0:T(8,128)(2,1)}, u32[]{:S(2)}, u32[]{:S(2)}) collective-permute-start(bf16[384,1024]{1,0:T(8,128)(2,1)} %get-tuple-element.149), channel_id=1, source_target_pairs={{0,2},{1,3},{2,0},{3,1},{4,6},{5,7},{6,4},{7,5},{8,10},{9,11},{10,... | collective-permute-start | bytes 2359304 | tf_op jit(solution)/shard_map/ppermute | solution.py:41
  227.2 8.5 %collective-permute-start.15 = (bf16[3,112,512]{2,1,0:T(8,128)(2,1)}, bf16[3,112,512]{2,1,0:T(8,128)(2,1)S(1)}, u32[]{:S(2)}, u32[]{:S(2)}) collective-permute-start(bf16[3,112,512]{2,1,0:T(8,128)(2,1)} %take_pieces.15), channel_id=1, source_target_pairs={{0,16},{8,24},{16,0},{24,8},{32,48},{40,56},{48,32},{56,40},{64,80... | collective-permute-start | bytes 1032200 | tf_op jit(solution)/shard_map/ppermute | solution.py:48
  235.7 23.1 %collective-permute-start.17 = (bf16[384,896]{1,0:T(8,128)(2,1)}, bf16[384,896]{1,0:T(8,128)(2,1)}, u32[]{:S(2)}, u32[]{:S(2)}) collective-permute-start(bf16[384,896]{1,0:T(8,128)(2,1)} %get-tuple-element.153), channel_id=1, source_target_pairs={{0,1},{1,2},{2,3},{3,0},{4,5},{5,6},{6,7},{7,4},{8,9},{9,10},{10,1... | collective-permute-start | bytes 2064392 | tf_op jit(solution)/shard_map/ppermute | solution.py:41
  235.7 32.8 %collective-permute-start.18 = (bf16[384,896]{1,0:T(8,128)(2,1)}, bf16[384,896]{1,0:T(8,128)(2,1)}, u32[]{:S(2)}, u32[]{:S(2)}) collective-permute-start(bf16[384,896]{1,0:T(8,128)(2,1)} %get-tuple-element.155), channel_id=1, source_target_pairs={{0,2},{1,3},{2,0},{3,1},{4,6},{5,7},{6,4},{7,5},{8,10},{9,11},{10,... | collective-permute-start | bytes 2064392 | tf_op jit(solution)/shard_map/ppermute | solution.py:41
  240.2 29.3 %collective-permute-start.19 = (bf16[384,896]{1,0:T(8,128)(2,1)}, bf16[384,896]{1,0:T(8,128)(2,1)}, u32[]{:S(2)}, u32[]{:S(2)}) collective-permute-start(bf16[384,896]{1,0:T(8,128)(2,1)} %get-tuple-element.157), channel_id=1, source_target_pairs={{0,3},{1,0},{2,1},{3,2},{4,7},{5,4},{6,5},{7,6},{8,11},{9,8},{10,9... | collective-permute-start | bytes 2064392 | tf_op jit(solution)/shard_map/ppermute | solution.py:41
  251.1 45.2 %all-to-all-start.4 = ((bf16[8,3,112,512]{3,2,1,0:T(8,128)(2,1)}), bf16[8,3,112,512]{3,2,1,0:T(8,128)(2,1)}, u32[]{:S(2)}, u32[]{:S(2)}) async-start(bf16[8,3,112,512]{3,2,1,0:T(8,128)(2,1)} %get-tuple-element.196), calls=%async_computation.4 | async-start | bytes 5505024 | tf_op jit(solution)/shard_map/all_to_all | solution.py:52
  (8 other events, 131.0 us)
Sparse Core Ops, SparseCore 0:
  10.2 69.3 all-gather.7
  81.3 41.0 all-gather.9
  241.1 37.5 all-gather.11
